TPU v7x, 512 devices: a whole 4x8x8 slice. The times are simulated.
512 devices in a mesh: seq: 256 (over z, x, y_lo, core), head: 2 (over y_hi).
Axes of the slice: x: 4, y: 8 (y_hi: 2, y_lo: 4; y = y_hi * 4 + y_lo), z: 8, core: 2. Of those that a mesh axis runs over, the one named last changes fastest.
Arguments:
- queries: bfloat16 [65536, 2048], P('seq', 'head'), may hold values from -5 to 5
- key_vectors: bfloat16 [65536, 2048], P('seq', 'head'), may hold values from -5 to 5
- value_vectors: bfloat16 [65536, 2048], P('seq', 'head'), may hold values from -6 to 6
- norm_gain: float32 [2048], P('head'), may hold values from 0.5 to 1.5
- cotangent: bfloat16 [65536, 2048], P('seq', 'head'), may hold values from -6 to 6
Outputs:
- normed: bfloat16 [65536, 2048], P('seq', 'head')
- query_grad: bfloat16 [65536, 2048], P('seq', 'head')
- key_grad: bfloat16 [65536, 2048], P('seq', 'head')
- value_grad: bfloat16 [65536, 2048], P('seq', 'head')
All inputs are finite; a program needn't handle non-finite values.
Results may differ from a plain program's by a relative error of at most 0.008.
Values may be sent and summed in bfloat16 or wider, within the bound.
No kernel may reach another device: no remote copies, remote signals or barrier semaphores. Data moves between devices by JAX's collectives and lax.ppermute only.
A program may use at most 64 MiB of HBM per device.

v0:
```python
from functools import partial

import jax
import jax.numpy as jnp
from jax import lax
from jax.sharding import PartitionSpec as P

HEADS = 16
HDIM = 128
BLOCK = 16


def extended(x, sides, width):
    for axis, dim in sides:
        size, length = (lax.axis_size(axis), x.shape[dim])
        up = [(i, (i + 1) % size) for i in range(size - 1)]
        down = [(j, i) for i, j in up]
        last = lax.slice_in_dim(x, length - width, length, axis=dim)
        first = lax.slice_in_dim(x, 0, width, axis=dim)
        before = lax.ppermute(last, axis, up)
        after = lax.ppermute(first, axis, down)
        x = jnp.concatenate([before, x, after], axis=dim)
    return x


def passed_along(block, axis, distance):
    devices = range(lax.axis_size(axis))
    route = [(i - distance, i) for i in devices if i - distance in devices]
    return lax.ppermute(block, axis, route)


def pool_rows(stacked, factor, weight):
    shaped = stacked.reshape(stacked.shape[0], stacked.shape[1] // factor, factor, stacked.shape[2])
    return (jnp.sum(shaped, axis=2, dtype=jnp.float32) * weight).astype(jnp.bfloat16)


def unpool(grads, factor):
    spread = jnp.broadcast_to(
        grads[:, :, None, :], (grads.shape[0], grads.shape[1], factor, grads.shape[2])
    )
    return spread.reshape(grads.shape[0], grads.shape[1] * factor, grads.shape[2])


def key_masks(start_row, row_count, seq_total, rim_rows):
    query_pos = start_row + jnp.arange(row_count, dtype=jnp.int32)
    raw_pos = start_row - rim_rows + jnp.arange(row_count + 2 * rim_rows, dtype=jnp.int32)
    near_ok = jnp.abs(raw_pos[None, :] // rim_rows - query_pos[:, None] // rim_rows) <= 1
    near_ok = near_ok & (raw_pos >= 0)[None, :] & (raw_pos < seq_total)[None, :]
    middle_pos = (
        start_row // 4 - rim_rows + jnp.arange(row_count // 4 + 2 * rim_rows, dtype=jnp.int32)
    )
    middle_gap = middle_pos[None, :] // rim_rows - query_pos[:, None] // (4 * rim_rows)
    middle_ok = (
        (jnp.abs(middle_gap) == 1)
        & (middle_pos >= 0)[None, :]
        & (middle_pos < seq_total // 4)[None, :]
    )
    coarse_pos = (
        start_row // rim_rows
        - rim_rows
        + jnp.arange(row_count // rim_rows + 2 * rim_rows, dtype=jnp.int32)
    )
    coarse_gap = coarse_pos[None, :] // rim_rows - query_pos[:, None] // (rim_rows * rim_rows)
    coarse_ok = (
        (jnp.abs(coarse_gap) == 1)
        & (coarse_pos >= 0)[None, :]
        & (coarse_pos < seq_total // rim_rows)[None, :]
    )
    return jnp.concatenate([near_ok, middle_ok, coarse_ok], axis=1)


def attend(queries, near_ext, middle_ext, coarse_ext, key_mask):
    key_rows = jnp.concatenate([near_ext[0], middle_ext[0], coarse_ext[0]], axis=0)
    value_rows = jnp.concatenate([near_ext[1], middle_ext[1], coarse_ext[1]], axis=0)
    head_count = queries.shape[1] // HDIM
    query_heads = queries.astype(jnp.float32).reshape(queries.shape[0], head_count, HDIM)
    key_heads = key_rows.astype(jnp.float32).reshape(key_rows.shape[0], head_count, HDIM)
    value_heads = value_rows.astype(jnp.float32).reshape(value_rows.shape[0], head_count, HDIM)
    scores = jnp.einsum(
        "qhd,khd->hqk", query_heads, key_heads, precision=lax.Precision.HIGHEST
    ) * HDIM ** (-0.5)
    scores = jnp.where(key_mask[None, :, :], scores, -1e30)
    highest = jnp.max(scores, axis=2, keepdims=True)
    lifted = jnp.exp(scores - highest)
    weights = lifted / jnp.sum(lifted, axis=2, keepdims=True)
    rounded = lax.optimization_barrier(weights.astype(jnp.bfloat16)).astype(jnp.float32)
    mixed_heads = jnp.einsum("hqk,khd->qhd", rounded, value_heads, precision=lax.Precision.HIGHEST)
    return mixed_heads.reshape(queries.shape[0], head_count * HDIM)


def settle(grad_ext, from_below, from_above, rim_rows):
    inner_rows = grad_ext[:, rim_rows:-rim_rows].astype(jnp.float32)
    span_rows = inner_rows.shape[1]
    inner_rows = inner_rows + jnp.pad(
        from_below.astype(jnp.float32), ((0, 0), (0, span_rows - rim_rows), (0, 0))
    )
    return inner_rows + jnp.pad(
        from_above.astype(jnp.float32), ((0, 0), (span_rows - rim_rows, 0), (0, 0))
    )


def extend_level(level_rows, rim_rows):
    return extended(level_rows, (("seq", 1),), rim_rows)


def return_level(grad_ext, rim_rows):
    from_above = passed_along(grad_ext[:, :rim_rows], "seq", -1)
    from_below = passed_along(grad_ext[:, -rim_rows:], "seq", 1)
    return settle(grad_ext, from_below, from_above, rim_rows)


def local(queries, key_vectors, value_vectors, norm_gain, cotangent):
    row_count = queries.shape[0]
    rim_rows = BLOCK
    feat_all = HEADS * HDIM
    start_row = lax.axis_index("seq") * row_count
    seq_total = row_count * lax.axis_size("seq")
    stacked = jnp.stack([key_vectors, value_vectors])
    key_mask = key_masks(start_row, row_count, seq_total, rim_rows)
    near_ext = extend_level(stacked, rim_rows)
    middle_ext = extend_level(pool_rows(stacked, 4, 0.5), rim_rows)
    coarse_ext = extend_level(pool_rows(stacked, rim_rows, 0.25), rim_rows)
    attended, pullback = jax.vjp(
        partial(attend, key_mask=key_mask), queries, near_ext, middle_ext, coarse_ext
    )
    scaled = cotangent.astype(jnp.float32) * norm_gain[None, :]
    squares, crossed = lax.psum(
        (jnp.sum(attended * attended, axis=1), jnp.sum(scaled * attended, axis=1)), "head"
    )
    factor = lax.rsqrt(squares / feat_all + 1e-06)
    normed = (norm_gain[None, :] * attended * factor[:, None]).astype(jnp.bfloat16)
    grad_out = (
        factor[:, None] * scaled
        - attended * (factor * factor * factor * crossed / feat_all)[:, None]
    )
    query_grad, near_grad, middle_grad, coarse_grad = pullback(grad_out)
    own_grad = return_level(near_grad, rim_rows)
    own_grad = own_grad + unpool(return_level(middle_grad, rim_rows), 4) * 0.5
    own_grad = own_grad + unpool(return_level(coarse_grad, rim_rows), rim_rows) * 0.25
    return (normed, query_grad, own_grad[0].astype(jnp.bfloat16), own_grad[1].astype(jnp.bfloat16))


def solution(mesh):
    in_specs = (P("seq", "head"), P("seq", "head"), P("seq", "head"), P("head"), P("seq", "head"))
    out_specs = (P("seq", "head"), P("seq", "head"), P("seq", "head"), P("seq", "head"))
    return jax.shard_map(local, mesh=mesh, in_specs=in_specs, out_specs=out_specs, check_vma=False)
```

profile of v0, /device:TPU:255, one launch (start us, length us, event | category | flops | bytes accessed | tf_op | source)
XLA Modules:
  0.0 116.2 jit_solution(2236354083389387858)
XLA Ops:
  0.7 1.7 %convert_reduce_fusion.1 = f32[2,16,1024]{2,1,0:T(8,128)S(1)} fusion(bf16[1,16,16,1024]{3,2,1,0:T(8,128)(2,1)} %bitcast.94, bf16[1,16,16,1024]{3,2,1,0:T(8,128)(2,1)} %bitcast.97), kind=kLoop, calls=%fused_computation.17 | loop fusion | flops 1540096 | bytes 1179648 | tf_op jit(solution)/shard_map/reduce_sum | solution.py:34
  2.4 2.6 %collective-permute-start.5 = (bf16[2,16,1024]{2,1,0:T(8,128)(2,1)S(1)}, bf16[2,16,1024]{2,1,0:T(8,128)(2,1)S(1)}, u32[]{:S(2)}, u32[]{:S(2)}) collective-permute-start(bf16[2,16,1024]{2,1,0:T(8,128)(2,1)S(1)} %multiply_convert_fusion.2), channel_id=1, source_target_pairs={{2,0},{4,2},{6,4},{8,6},{10,8},{12,10},{14,12},{16,14},{18,16},{20... | collective-permute-start | bytes 196616 | tf_op jit(solution)/shard_map/ppermute | solution.py:21
  5.0 9.0 %collective-permute-start.4 = (bf16[2,16,1024]{2,1,0:T(8,128)(2,1)S(1)}, bf16[2,16,1024]{2,1,0:T(8,128)(2,1)S(1)}, u32[]{:S(2)}, u32[]{:S(2)}) collective-permute-start(bf16[2,16,1024]{2,1,0:T(8,128)(2,1)S(1)} %multiply_convert_fusion.2), channel_id=1, source_target_pairs={{0,2},{2,4},{4,6},{6,8},{8,10},{10,12},{12,14},{14,16},{16,18},{18... | collective-permute-start | bytes 196616 | tf_op jit(solution)/shard_map/ppermute | solution.py:20
  14.8 1.9 %collective-permute-start = (bf16[2,16,1024]{2,1,0:T(8,128)(2,1)S(1)}, bf16[2,16,1024]{2,1,0:T(8,128)(2,1)S(1)}, u32[]{:S(2)}, u32[]{:S(2)}) collective-permute-start(bf16[2,16,1024]{2,1,0:T(8,128)(2,1)S(1)} %get-tuple-element.27), channel_id=1, source_target_pairs={{0,2},{2,4},{4,6},{6,8},{8,10},{10,12},{12,14},{14,16},{16,18},{18... | collective-permute-start | bytes 196616 | tf_op jit(solution)/shard_map/ppermute | solution.py:20
  19.7 1.9 %collective-permute-start.2 = (bf16[2,16,1024]{2,1,0:T(8,128)(2,1)S(1)}, bf16[2,16,1024]{2,1,0:T(8,128)(2,1)S(1)}, u32[]{:S(2)}, u32[]{:S(2)}) collective-permute-start(bf16[2,16,1024]{2,1,0:T(8,128)(2,1)S(1)} %get-tuple-element.33), channel_id=1, source_target_pairs={{0,2},{2,4},{4,6},{6,8},{8,10},{10,12},{12,14},{14,16},{16,18},{18... | collective-permute-start | bytes 196616 | tf_op jit(solution)/shard_map/ppermute | solution.py:20
  21.6 2.4 %collective-permute-start.3 = (bf16[2,16,1024]{2,1,0:T(8,128)(2,1)S(1)}, bf16[2,16,1024]{2,1,0:T(8,128)(2,1)S(1)}, u32[]{:S(2)}, u32[]{:S(2)}) collective-permute-start(bf16[2,16,1024]{2,1,0:T(8,128)(2,1)S(1)} %get-tuple-element.34), channel_id=1, source_target_pairs={{2,0},{4,2},{6,4},{8,6},{10,8},{12,10},{14,12},{16,14},{18,16},{20... | collective-permute-start | bytes 196616 | tf_op jit(solution)/shard_map/ppermute | solution.py:21
  24.6 3.6 %collective-permute-start.1 = (bf16[2,16,1024]{2,1,0:T(8,128)(2,1)S(1)}, bf16[2,16,1024]{2,1,0:T(8,128)(2,1)S(1)}, u32[]{:S(2)}, u32[]{:S(2)}) collective-permute-start(bf16[2,16,1024]{2,1,0:T(8,128)(2,1)S(1)} %get-tuple-element.28), channel_id=1, source_target_pairs={{2,0},{4,2},{6,4},{8,6},{10,8},{12,10},{14,12},{16,14},{18,16},{20... | collective-permute-start | bytes 196616 | tf_op jit(solution)/shard_map/ppermute | solution.py:21
  28.3 4.9 %collective-permute-done.3 = bf16[2,16,1024]{2,1,0:T(8,128)(2,1)S(1)} collective-permute-done((bf16[2,16,1024]{2,1,0:T(8,128)(2,1)S(1)}, bf16[2,16,1024]{2,1,0:T(8,128)(2,1)S(1)}, u32[]{:S(2)}, u32[]{:S(2)}) %collective-permute-start.3) | collective-permute-done | bytes 65568 | tf_op jit(solution)/shard_map/ppermute | solution.py:21
  33.4 2.8 %collective-permute-done.1 = bf16[2,16,1024]{2,1,0:T(8,128)(2,1)S(1)} collective-permute-done((bf16[2,16,1024]{2,1,0:T(8,128)(2,1)S(1)}, bf16[2,16,1024]{2,1,0:T(8,128)(2,1)S(1)}, u32[]{:S(2)}, u32[]{:S(2)}) %collective-permute-start.1) | collective-permute-done | bytes 65568 | tf_op jit(solution)/shard_map/ppermute | solution.py:21
  39.1 2.4 %convert_reduce_fusion = (f32[8,256]{1,0:T(8,128)S(1)}, pred[8,256,432]{1,2,0:T(8,128)(4,1)}, bf16[8,256,432]{1,2,0:T(8,128)(2,1)S(1)}) fusion(f32[8,256]{1,0:T(8,128)S(1)} %get-tuple-element.41, f32[8,432,256]{2,1,0:T(8,128)S(1)} %get-tuple-element.42, pred[256,432]{0,1:T(8,128)(4,1)S(1)} %pad_add_fusion, f32[8,256]{1,0:T(8,128)S(1)} %fusion.23), kind=kLoop, calls=%fused_computation.8 | loop fusion | flops 7075840 | bytes 6328320 | tf_op jit(solution)/shard_map/jvp()/reduce_sum | solution.py:83
  46.2 7.9 %all-reduce.10 = (f32[256]{0:T(256)S(1)}, f32[256]{0:T(256)S(1)}) all-reduce(f32[256]{0:T(256)S(1)} %get-tuple-element.43, f32[256]{0:T(256)S(1)} %multiply_reduce_fusion), channel_id=1, replica_groups=mesh['seq'=256,'head'=2] {'head'}, use_global_device_ids=true, to_apply=%region_5.6 | all-reduce | flops 512 | bytes 4096 | tf_op jit(solution)/shard_map/psum | solution.py:127
  54.1 2.5 %multiply_subtract_fusion = (f32[256,1024]{1,0:T(8,128)}, bf16[256,1024]{1,0:T(8,128)(2,1)}) fusion(f32[256,1024]{1,0:T(8,128)S(1)} %copy.23, bf16[256,1024]{1,0:T(8,128)(2,1)} %param.9, f32[256]{0:T(256)S(1)} %get-tuple-element.39, f32[256]{0:T(256)S(1)} %get-tuple-element.40, f32[1024]{0:T(1024)S(1)} %copy-done.15), kind=kLoop, calls=%fused_computation.41 | loop fusion | flops 2097152 | bytes 3151872 | tf_op jit(solution)/shard_map/sub | solution.py:133
  59.8 1.6 %convolution_convert_fusion = bf16[8,256,432]{1,2,0:T(8,128)(2,1)S(1)} fusion(f32[8,128,256]{2,1,0:T(8,128)S(1)} %bitcast.93, bf16[432,8,128]{2,0,1:T(8,128)(2,1)S(1)} %copy-done.6), kind=kOutput, calls=%fused_computation.27 | convolution fusion | flops 1359839232 | bytes 3702784 | tf_op jit(solution)/shard_map/transpose(jvp(hqk,khd->qhd))/dot_general | solution.py:87
  63.9 3.3 %fusion.20 = bf16[8,256,128]{1,2,0:T(8,128)(2,1)} fusion(bf16[432,8,128]{2,0,1:T(8,128)(2,1)S(1)} %copy-done.10, f32[8,256,432]{1,2,0:T(8,128)S(1)} %get-tuple-element.15, pred[8,256,432]{1,2,0:T(8,128)(4,1)S(1)} %copy-done.12, f32[8,256]{1,0:T(8,128)S(1)} %negate_divide_fusion, pred[256,432]{0,1:T(8,128)(4,1)S(1)} %pad_add_fusion), kind=kOutput, calls=%fused_computation.36 | convolution fusion | flops 1362755584 | bytes 5951488 | tf_op jit(solution)/shard_map/transpose(jvp(qhd,khd->hqk))/dot_general | solution.py:79
  67.2 2.4 %fusion.19 = bf16[432,8,128]{2,0,1:T(8,128)(2,1)S(1)} fusion(f32[8,256,432]{1,2,0:T(8,128)S(1)} %get-tuple-element.15, pred[8,256,432]{1,2,0:T(8,128)(4,1)S(1)} %copy-done.12, f32[8,256]{1,0:T(8,128)S(1)} %negate_divide_fusion, pred[256,432]{0,1:T(8,128)(4,1)S(1)} %pad_add_fusion, bf16[256,1024]{1,0:T(8,128)(2,1)S(1)} %copy-done), kind=kOutput, calls=%fused_computation.35 | convolution fusion | flops 1362935808 | bytes 5951488 | tf_op jit(solution)/shard_map/transpose(jvp(qhd,khd->hqk))/dot_general | solution.py:79
  72.9 3.0 %collective-permute-start.10 = (bf16[2,16,1024]{2,1,0:T(8,128)(2,1)}, bf16[2,16,1024]{2,1,0:T(8,128)(2,1)}, u32[]{:S(2)}, u32[]{:S(2)}) collective-permute-start(bf16[2,16,1024]{2,1,0:T(8,128)(2,1)} %get-tuple-element.35), channel_id=1, source_target_pairs={{0,2},{2,4},{4,6},{6,8},{8,10},{10,12},{12,14},{14,16},{16,18},{18... | collective-permute-start | bytes 196616 | tf_op jit(solution)/shard_map/ppermute | solution.py:29
  75.9 2.1 %collective-permute-start.11 = (bf16[2,16,1024]{2,1,0:T(8,128)(2,1)}, bf16[2,16,1024]{2,1,0:T(8,128)(2,1)}, u32[]{:S(2)}, u32[]{:S(2)}) collective-permute-start(bf16[2,16,1024]{2,1,0:T(8,128)(2,1)} %get-tuple-element.36), channel_id=1, source_target_pairs={{2,0},{4,2},{6,4},{8,6},{10,8},{12,10},{14,12},{16,14},{18,16},{20... | collective-permute-start | bytes 196616 | tf_op jit(solution)/shard_map/ppermute | solution.py:29
  79.4 9.4 %collective-permute-start.8 = (bf16[2,16,1024]{2,1,0:T(8,128)(2,1)S(1)}, bf16[2,16,1024]{2,1,0:T(8,128)(2,1)S(1)}, u32[]{:S(2)}, u32[]{:S(2)}) collective-permute-start(bf16[2,16,1024]{2,1,0:T(8,128)(2,1)S(1)} %get-tuple-element.29), channel_id=1, source_target_pairs={{0,2},{2,4},{4,6},{6,8},{8,10},{10,12},{12,14},{14,16},{16,18},{18... | collective-permute-start | bytes 196616 | tf_op jit(solution)/shard_map/ppermute | solution.py:29
  88.9 1.9 %collective-permute-start.9 = (bf16[2,16,1024]{2,1,0:T(8,128)(2,1)S(1)}, bf16[2,16,1024]{2,1,0:T(8,128)(2,1)S(1)}, u32[]{:S(2)}, u32[]{:S(2)}) collective-permute-start(bf16[2,16,1024]{2,1,0:T(8,128)(2,1)S(1)} %get-tuple-element.30), channel_id=1, source_target_pairs={{2,0},{4,2},{6,4},{8,6},{10,8},{12,10},{14,12},{16,14},{18,16},{20... | collective-permute-start | bytes 196616 | tf_op jit(solution)/shard_map/ppermute | solution.py:29
  91.5 9.6 %collective-permute-start.6 = (bf16[2,16,1024]{2,1,0:T(8,128)(2,1)}, bf16[2,16,1024]{2,1,0:T(8,128)(2,1)S(1)}, u32[]{:S(2)}, u32[]{:S(2)}) collective-permute-start(bf16[2,16,1024]{2,1,0:T(8,128)(2,1)} %get-tuple-element.19), channel_id=1, source_target_pairs={{0,2},{2,4},{4,6},{6,8},{8,10},{10,12},{12,14},{14,16},{16,18},{18... | collective-permute-start | bytes 196616 | tf_op jit(solution)/shard_map/ppermute | solution.py:29
  101.1 1.9 %collective-permute-start.7 = (bf16[2,16,1024]{2,1,0:T(8,128)(2,1)}, bf16[2,16,1024]{2,1,0:T(8,128)(2,1)}, u32[]{:S(2)}, u32[]{:S(2)}) collective-permute-start(bf16[2,16,1024]{2,1,0:T(8,128)(2,1)} %get-tuple-element.20), channel_id=1, source_target_pairs={{2,0},{4,2},{6,4},{8,6},{10,8},{12,10},{14,12},{16,14},{18,16},{20... | collective-permute-start | bytes 196616 | tf_op jit(solution)/shard_map/ppermute | solution.py:29
  105.3 1.7 %mul.145 = f32[2,256,1024]{2,1,0:T(8,128)} reshape(f32[2,64,4,1024]{3,2,1,0:T(4,128)S(1)} %broadcast_in_dim.45) | data formatting | bytes 4194304 | tf_op jit(solution)/shard_map/mul | solution.py:138
  107.0 6.0 %collective-permute-done.7 = bf16[2,16,1024]{2,1,0:T(8,128)(2,1)} collective-permute-done((bf16[2,16,1024]{2,1,0:T(8,128)(2,1)}, bf16[2,16,1024]{2,1,0:T(8,128)(2,1)}, u32[]{:S(2)}, u32[]{:S(2)}) %collective-permute-start.7) | collective-permute-done | bytes 65568 | tf_op jit(solution)/shard_map/ppermute | solution.py:29
  113.1 2.1 %fusion.8 = bf16[2,256,1024]{2,1,0:T(8,128)(2,1)S(1)} fusion(f32[2,256,1024]{2,1,0:T(8,128)} %mul.145, bf16[1,288,1024]{2,1,0:T(8,128)(2,1)} %copy-done.7, bf16[1,288,1024]{2,1,0:T(8,128)(2,1)S(1)} %broadcast_in_dim.42, f32[2,16,1024]{2,1,0:T(8,128)S(1)} %copy-done.13, bf16[2,16,1024]{2,1,0:T(8,128)(2,1)} %collective-permute-done.7, ...), kind=kLoop, calls=%fused_computation.16 | loop fusion | flops 5767168 | bytes 4587520 | tf_op jit(solution)/shard_map/convert.9
  (120 shorter events, 25.8 us)
Async XLA Ops:
  0.6 37.0 %copy-start = (bf16[256,1024]{1,0:T(8,128)(2,1)S(1)}, bf16[256,1024]{1,0:T(8,128)(2,1)}, u32[]{:S(2)}) copy-start(bf16[256,1024]{1,0:T(8,128)(2,1)} %param.5) | copy-start | bytes 1572868
  0.6 17.3 %copy-start.3 = (bf16[256,1024]{1,0:T(8,128)(2,1)S(1)}, bf16[256,1024]{1,0:T(8,128)(2,1)}, u32[]{:S(2)}) copy-start(bf16[256,1024]{1,0:T(8,128)(2,1)} %param.7) | copy-start | bytes 1572868
  2.4 30.9 %collective-permute-start.5 = (bf16[2,16,1024]{2,1,0:T(8,128)(2,1)S(1)}, bf16[2,16,1024]{2,1,0:T(8,128)(2,1)S(1)}, u32[]{:S(2)}, u32[]{:S(2)}) collective-permute-start(bf16[2,16,1024]{2,1,0:T(8,128)(2,1)S(1)} %multiply_convert_fusion.2), channel_id=1, source_target_pairs={{2,0},{4,2},{6,4},{8,6},{10,8},{12,10},{14,12},{16,14},{18,16},{20... | collective-permute-start | bytes 196616 | tf_op jit(solution)/shard_map/ppermute | solution.py:21
  5.0 28.3 %collective-permute-start.4 = (bf16[2,16,1024]{2,1,0:T(8,128)(2,1)S(1)}, bf16[2,16,1024]{2,1,0:T(8,128)(2,1)S(1)}, u32[]{:S(2)}, u32[]{:S(2)}) collective-permute-start(bf16[2,16,1024]{2,1,0:T(8,128)(2,1)S(1)} %multiply_convert_fusion.2), channel_id=1, source_target_pairs={{0,2},{2,4},{4,6},{6,8},{8,10},{10,12},{12,14},{14,16},{16,18},{18... | collective-permute-start | bytes 196616 | tf_op jit(solution)/shard_map/ppermute | solution.py:20
  14.8 18.6 %collective-permute-start = (bf16[2,16,1024]{2,1,0:T(8,128)(2,1)S(1)}, bf16[2,16,1024]{2,1,0:T(8,128)(2,1)S(1)}, u32[]{:S(2)}, u32[]{:S(2)}) collective-permute-start(bf16[2,16,1024]{2,1,0:T(8,128)(2,1)S(1)} %get-tuple-element.27), channel_id=1, source_target_pairs={{0,2},{2,4},{4,6},{6,8},{8,10},{10,12},{12,14},{14,16},{16,18},{18... | collective-permute-start | bytes 196616 | tf_op jit(solution)/shard_map/ppermute | solution.py:20
  18.0 18.3 %copy-start.4 = (bf16[256,1024]{1,0:T(8,128)(2,1)S(1)}, bf16[256,1024]{1,0:T(8,128)(2,1)}, u32[]{:S(2)}) copy-start(bf16[256,1024]{1,0:T(8,128)(2,1)} %param.6) | copy-start | bytes 1572868
  19.7 4.9 %collective-permute-start.2 = (bf16[2,16,1024]{2,1,0:T(8,128)(2,1)S(1)}, bf16[2,16,1024]{2,1,0:T(8,128)(2,1)S(1)}, u32[]{:S(2)}, u32[]{:S(2)}) collective-permute-start(bf16[2,16,1024]{2,1,0:T(8,128)(2,1)S(1)} %get-tuple-element.33), channel_id=1, source_target_pairs={{0,2},{2,4},{4,6},{6,8},{8,10},{10,12},{12,14},{14,16},{16,18},{18... | collective-permute-start | bytes 196616 | tf_op jit(solution)/shard_map/ppermute | solution.py:20
  21.6 11.6 %collective-permute-start.3 = (bf16[2,16,1024]{2,1,0:T(8,128)(2,1)S(1)}, bf16[2,16,1024]{2,1,0:T(8,128)(2,1)S(1)}, u32[]{:S(2)}, u32[]{:S(2)}) collective-permute-start(bf16[2,16,1024]{2,1,0:T(8,128)(2,1)S(1)} %get-tuple-element.34), channel_id=1, source_target_pairs={{2,0},{4,2},{6,4},{8,6},{10,8},{12,10},{14,12},{16,14},{18,16},{20... | collective-permute-start | bytes 196616 | tf_op jit(solution)/shard_map/ppermute | solution.py:21
  24.6 11.6 %collective-permute-start.1 = (bf16[2,16,1024]{2,1,0:T(8,128)(2,1)S(1)}, bf16[2,16,1024]{2,1,0:T(8,128)(2,1)S(1)}, u32[]{:S(2)}, u32[]{:S(2)}) collective-permute-start(bf16[2,16,1024]{2,1,0:T(8,128)(2,1)S(1)} %get-tuple-element.28), channel_id=1, source_target_pairs={{2,0},{4,2},{6,4},{8,6},{10,8},{12,10},{14,12},{16,14},{18,16},{20... | collective-permute-start | bytes 196616 | tf_op jit(solution)/shard_map/ppermute | solution.py:21
  38.3 3.2 %copy-start.1 = (f32[8,432,256]{2,1,0:T(8,128)}, f32[8,432,256]{2,1,0:T(8,128)S(1)}, u32[]{:S(2)}) copy-start(f32[8,432,256]{2,1,0:T(8,128)S(1)} %get-tuple-element.42) | copy-start | bytes 10616836
  41.7 3.3 %copy-start.15 = (f32[1024]{0:T(1024)S(1)}, f32[1024]{0:T(1024)}, u32[]{:S(2)}) copy-start(f32[1024]{0:T(1024)} %param.8) | copy-start | bytes 12292
  58.2 3.2 %copy-start.2 = (f32[8,432,256]{2,1,0:T(8,128)S(1)}, f32[8,432,256]{2,1,0:T(8,128)}, u32[]{:S(2)}) copy-start(f32[8,432,256]{2,1,0:T(8,128)} %copy-done.1) | copy-start | bytes 10616836
  59.8 10.0 %copy-start.8 = (bf16[432,8,128]{2,0,1:T(8,128)(2,1)}, bf16[432,8,128]{2,0,1:T(8,128)(2,1)S(1)}, u32[]{:S(2)}) copy-start(bf16[432,8,128]{2,0,1:T(8,128)(2,1)S(1)} %fusion.18) | copy-start | bytes 2654212
  70.6 7.9 %slice-start.2 = ((bf16[432,8,128]{2,0,1:T(8,128)(2,1)}), bf16[96,8,128]{2,0,1:T(8,128)(2,1)S(1)}, s32[]{:S(2)}) async-start(bf16[432,8,128]{2,0,1:T(8,128)(2,1)} %copy-done.11), calls=%async_computation.2 | async-start | bytes 393216 | tf_op jit(solution)/shard_map/transpose(jvp())/split | solution.py:73
  70.6 8.1 %slice-start.1 = ((bf16[432,8,128]{2,0,1:T(8,128)(2,1)}), bf16[288,8,128]{2,0,1:T(8,128)(2,1)S(1)}, s32[]{:S(2)}) async-start(bf16[432,8,128]{2,0,1:T(8,128)(2,1)} %copy-done.8), calls=%async_computation.1 | async-start | bytes 1179648 | tf_op jit(solution)/shard_map/transpose(jvp())/split | solution.py:74
  72.0 7.2 %slice-start = ((bf16[432,8,128]{2,0,1:T(8,128)(2,1)}), bf16[96,8,128]{2,0,1:T(8,128)(2,1)S(1)}, s32[]{:S(2)}) async-start(bf16[432,8,128]{2,0,1:T(8,128)(2,1)} %copy-done.8), calls=%async_computation | async-start | bytes 393216 | tf_op jit(solution)/shard_map/transpose(jvp())/split | solution.py:74
  72.9 28.3 %collective-permute-start.10 = (bf16[2,16,1024]{2,1,0:T(8,128)(2,1)}, bf16[2,16,1024]{2,1,0:T(8,128)(2,1)}, u32[]{:S(2)}, u32[]{:S(2)}) collective-permute-start(bf16[2,16,1024]{2,1,0:T(8,128)(2,1)} %get-tuple-element.35), channel_id=1, source_target_pairs={{0,2},{2,4},{4,6},{6,8},{8,10},{10,12},{12,14},{14,16},{16,18},{18... | collective-permute-start | bytes 196616 | tf_op jit(solution)/shard_map/ppermute | solution.py:29
  75.9 27.2 %collective-permute-start.11 = (bf16[2,16,1024]{2,1,0:T(8,128)(2,1)}, bf16[2,16,1024]{2,1,0:T(8,128)(2,1)}, u32[]{:S(2)}, u32[]{:S(2)}) collective-permute-start(bf16[2,16,1024]{2,1,0:T(8,128)(2,1)} %get-tuple-element.36), channel_id=1, source_target_pairs={{2,0},{4,2},{6,4},{8,6},{10,8},{12,10},{14,12},{16,14},{18,16},{20... | collective-permute-start | bytes 196616 | tf_op jit(solution)/shard_map/ppermute | solution.py:29
  79.2 25.4 %copy-start.7 = (bf16[1,288,1024]{2,1,0:T(8,128)(2,1)}, bf16[1,288,1024]{2,1,0:T(8,128)(2,1)S(1)}, u32[]{:S(2)}) copy-start(bf16[1,288,1024]{2,1,0:T(8,128)(2,1)S(1)} %broadcast_in_dim.41) | copy-start | bytes 1769476
  79.4 25.2 %collective-permute-start.8 = (bf16[2,16,1024]{2,1,0:T(8,128)(2,1)S(1)}, bf16[2,16,1024]{2,1,0:T(8,128)(2,1)S(1)}, u32[]{:S(2)}, u32[]{:S(2)}) collective-permute-start(bf16[2,16,1024]{2,1,0:T(8,128)(2,1)S(1)} %get-tuple-element.29), channel_id=1, source_target_pairs={{0,2},{2,4},{4,6},{6,8},{8,10},{10,12},{12,14},{14,16},{16,18},{18... | collective-permute-start | bytes 196616 | tf_op jit(solution)/shard_map/ppermute | solution.py:29
  88.9 15.8 %collective-permute-start.9 = (bf16[2,16,1024]{2,1,0:T(8,128)(2,1)S(1)}, bf16[2,16,1024]{2,1,0:T(8,128)(2,1)S(1)}, u32[]{:S(2)}, u32[]{:S(2)}) collective-permute-start(bf16[2,16,1024]{2,1,0:T(8,128)(2,1)S(1)} %get-tuple-element.30), channel_id=1, source_target_pairs={{2,0},{4,2},{6,4},{8,6},{10,8},{12,10},{14,12},{16,14},{18,16},{20... | collective-permute-start | bytes 196616 | tf_op jit(solution)/shard_map/ppermute | solution.py:29
  91.5 15.6 %collective-permute-start.6 = (bf16[2,16,1024]{2,1,0:T(8,128)(2,1)}, bf16[2,16,1024]{2,1,0:T(8,128)(2,1)S(1)}, u32[]{:S(2)}, u32[]{:S(2)}) collective-permute-start(bf16[2,16,1024]{2,1,0:T(8,128)(2,1)} %get-tuple-element.19), channel_id=1, source_target_pairs={{0,2},{2,4},{4,6},{6,8},{8,10},{10,12},{12,14},{14,16},{16,18},{18... | collective-permute-start | bytes 196616 | tf_op jit(solution)/shard_map/ppermute | solution.py:29
  101.1 11.9 %collective-permute-start.7 = (bf16[2,16,1024]{2,1,0:T(8,128)(2,1)}, bf16[2,16,1024]{2,1,0:T(8,128)(2,1)}, u32[]{:S(2)}, u32[]{:S(2)}) collective-permute-start(bf16[2,16,1024]{2,1,0:T(8,128)(2,1)} %get-tuple-element.20), channel_id=1, source_target_pairs={{2,0},{4,2},{6,4},{8,6},{10,8},{12,10},{14,12},{16,14},{18,16},{20... | collective-permute-start | bytes 196616 | tf_op jit(solution)/shard_map/ppermute | solution.py:29
  104.7 8.3 %copy-start.13 = (f32[2,16,1024]{2,1,0:T(8,128)S(1)}, f32[2,16,1024]{2,1,0:T(8,128)}, u32[]{:S(2)}) copy-start(f32[2,16,1024]{2,1,0:T(8,128)} %add_multiply_fusion.1) | copy-start | bytes 393220
  (7 other events, 9.0 us)
where the time goes:
time: 117 us; the launch traced here: 116 us
  starting transfers between devices  49.5 us (42%)
  other arithmetic  18.8 us (16%)
  waiting for transfers between devices  13.8 us (12%)
  local copies, waits for them, and re-layouts  13.6 us (12%)
  matrix products  11.1 us (9%)
  blocking collectives  7.89 us (7%)
  between operations  1.47 us (1%)
    ppermute x6, starting transfers between devices, passed_along(): return lax.ppermute(block, axis, route)  28.1 us
    ppermute x3, starting transfers between devices, extended(): before = lax.ppermute(last, axis, up)  12.8 us
    ppermute x3, starting transfers between devices, extended(): after = lax.ppermute(first, axis, down)  8.63 us
    psum x1, blocking collectives, local(): lax.psum((jnp.sum(attended * attended, axis=1), jnp.sum(scaled * attended...  7.89 us
    ppermute x3, waiting for transfers between devices, extended(): after = lax.ppermute(first, axis, down)  7.75 us
    dot_general x3, matrix products, attend(): jnp.einsum('qhd,khd->hqk', query_heads, key_heads, precision=lax.Precisio...  6.41 us
    ppermute x6, waiting for transfers between devices, passed_along(): return lax.ppermute(block, axis, route)  6.04 us
    dot_general x3, matrix products, attend(): jnp.einsum('hqk,khd->qhd', rounded, value_heads, precision=lax.Precision....  4.66 us
  transfers between devices with their start and end apart: 12, of which 3 were waited for; matrix products, arithmetic and copies ran while one was open for 9% of the time, Pallas kernels for 0%

commit v1 on v0

v1 whole, which is shorter than its diff:
```python
from functools import partial

import jax
import jax.numpy as jnp
from jax import lax
from jax.experimental import pallas as pl
from jax.experimental.pallas import tpu as pltpu
from jax.sharding import PartitionSpec as P

HEADS = 16
HDIM = 128
BLOCK = 16
SCALE = HDIM**-0.5
F32 = jnp.float32
BF16 = jnp.bfloat16

SIDE = 3 * BLOCK
OWN_RAW = 9 * BLOCK
OWN_MID = 3 * BLOCK
OWN = OWN_RAW + OWN_MID
WINDOW = SIDE + OWN + BLOCK
GROUP = 128


def dot(a, b, ca, cb):
    return lax.dot_general(a, b, (((ca,), (cb,)), ((), ())), preferred_element_type=F32)


def head_cols(h):
    return pl.ds(h * HDIM, HDIM)


def pool_matrix(rows):
    shape = (rows // 4 + rows // 16, rows)
    out_row = lax.broadcasted_iota(jnp.int32, shape, 0)
    row = lax.broadcasted_iota(jnp.int32, shape, 1)
    middle = (row // 4 == out_row).astype(F32) * 0.5
    coarse = (row // 16 == out_row - rows // 4).astype(F32) * 0.25
    return jnp.where(out_row < rows // 4, middle, coarse).astype(BF16)


def pack_kernel(where_ref, k_ref, v_ref, far_ref, near_ref, mid_ref):
    rows = k_ref.shape[0]
    mids = rows // 4
    parity = where_ref[0] % 2
    pool = pool_matrix(rows)
    far_raw = pl.multiple_of(parity * (rows - BLOCK), BLOCK)
    near_raw = pl.multiple_of((1 - parity) * (rows - BLOCK), BLOCK)
    far_mid = pl.multiple_of(parity * (mids - BLOCK), BLOCK)
    near_mid = pl.multiple_of((1 - parity) * (mids - BLOCK), BLOCK)
    for i, ref in enumerate((k_ref, v_ref)):
        pooled = dot(pool, ref[...], 1, 0).astype(BF16)
        mid_ref[i] = pooled[:mids]
        base = i * SIDE
        for out_ref, raw_at, mid_at in ((far_ref, far_raw, far_mid), (near_ref, near_raw, near_mid)):
            out_ref[base : base + BLOCK] = ref[pl.ds(raw_at, BLOCK)]
            out_ref[base + BLOCK : base + 2 * BLOCK] = mid_ref[i, pl.ds(mid_at, BLOCK)]
            out_ref[base + 2 * BLOCK : base + 3 * BLOCK] = pooled[mids:]


def place_sides(parity, far_ref, near_ref, side_ref):
    @pl.when(parity == 0)
    def _():
        side_ref[0] = far_ref[...]
        side_ref[1] = near_ref[...]

    @pl.when(parity == 1)
    def _():
        side_ref[0] = near_ref[...]
        side_ref[1] = far_ref[...]


def window(i, g, cols, side_ref, raw_ref, mid_ref):
    raw_at, mid_at = (g * (raw_ref.shape[0] - OWN_RAW), g * (mid_ref.shape[1] - OWN_MID))
    base = i * SIDE
    return jnp.concatenate(
        [
            side_ref[g, base : base + SIDE, cols],
            raw_ref[raw_at : raw_at + OWN_RAW, cols],
            mid_ref[i, mid_at : mid_at + OWN_MID, cols],
            side_ref[1 - g, base + 2 * BLOCK : base + SIDE, cols],
        ],
        axis=0,
    )


def allowed(g, has_below, has_above):
    shape = (WINDOW, GROUP)
    kb = lax.broadcasted_iota(jnp.int32, shape, 0) // BLOCK
    qb = lax.broadcasted_iota(jnp.int32, shape, 1) // BLOCK
    qm = qb // 4
    raw_gap = kb - 3 - g - qb
    mid_gap = kb - 12 - g - qm
    edge_raw = qb == (7 if g else 0)
    edge_mid = qm == (1 if g else 0)
    one = jnp.ones(shape, jnp.int32)
    none = jnp.zeros(shape, jnp.int32)
    own = jnp.where(kb < 12, jnp.where(jnp.abs(raw_gap) <= 1, one, none), jnp.where(jnp.abs(mid_gap) == 1, one, none))
    side = jnp.where(kb == 0, jnp.where(edge_raw, one, none), jnp.where(kb == 1, jnp.where(edge_mid, one, none), one))
    valid_side, valid_other = (has_above, has_below) if g else (has_below, has_above)
    return jnp.where(kb < 3, side * valid_side, jnp.where(kb == 15, one * valid_other, own))


def forward_kernel(
    where_ref, q_ref, k_ref, v_ref, mid_ref, far_ref, near_ref, gain_ref, cot_ref, w_ref, att_ref, sums_ref, side_ref, bias_ref
):
    place_sides(where_ref[0] % 2, far_ref, near_ref, side_ref)
    for g in range(2):
        ok = allowed(g, where_ref[1], where_ref[2])
        bias_ref[g] = jnp.where(ok == 1, 0.0, -1e30)
    for g in range(2):
        rows = slice(g * GROUP, (g + 1) * GROUP)
        squares = jnp.zeros((GROUP, HDIM), F32)
        crossed = jnp.zeros((GROUP, HDIM), F32)
        for h in range(8):
            cols = slice(h * HDIM, (h + 1) * HDIM)
            keys = window(0, g, cols, side_ref, k_ref, mid_ref)
            values = window(1, g, cols, side_ref, v_ref, mid_ref)
            scores = dot(keys, q_ref[rows, cols], 1, 1) * SCALE + bias_ref[g]
            lifted = jnp.exp(scores - jnp.max(scores, axis=0, keepdims=True))
            weights = lifted * (1.0 / jnp.sum(lifted, axis=0, keepdims=True))
            w_ref[g, h] = weights
            mixed = dot(weights.astype(BF16), values, 0, 0)
            att_ref[rows, cols] = mixed
            squares += mixed * mixed
            crossed += mixed * (cot_ref[rows, cols].astype(F32) * gain_ref[:, cols])
        sums_ref[0:1, rows] = jnp.sum(squares.T, axis=0, keepdims=True)
        sums_ref[1:2, rows] = jnp.sum(crossed.T, axis=0, keepdims=True)


def row_factors(sums_ref, others_ref):
    feat_all = HEADS * HDIM
    totals = sums_ref[...] + others_ref[...]
    factor = lax.rsqrt(totals[0:1] / feat_all + 1e-06)
    cross = factor * factor * factor * totals[1:2] / feat_all
    both = jnp.concatenate([factor, cross, jnp.zeros((6, factor.shape[1]), F32)], axis=0)
    columns = both.T
    return columns[:, 0:1], columns[:, 1:2]


def pieces_kernel(
    where_ref, q_ref, v_ref, mid_ref, far_ref, near_ref, gain_ref, cot_ref, w_ref, att_ref, sums_ref, others_ref,
    far_out, near_out, ds_ref, dout_ref, side_ref, piece_ref,
):
    parity = where_ref[0] % 2
    place_sides(parity, far_ref, near_ref, side_ref)
    factor, cross = row_factors(sums_ref, others_ref)
    for h in range(8):
        cols = slice(h * HDIM, (h + 1) * HDIM)
        remote = []
        for g in range(2):
            rows = slice(g * GROUP, (g + 1) * GROUP)
            scaled = cot_ref[rows, cols].astype(F32) * gain_ref[:, cols]
            grad_out = (factor[rows] * scaled - cross[rows] * att_ref[rows, cols]).astype(BF16)
            dout_ref[rows, cols] = grad_out
            values = window(1, g, cols, side_ref, v_ref, mid_ref)
            grad_w = dot(values, grad_out, 1, 1)
            weights = w_ref[g, h]
            middle = jnp.sum(weights * grad_w, axis=0, keepdims=True)
            ds = (weights * (grad_w - middle) * SCALE).astype(BF16)
            ds_ref[g, h] = ds
            low = jnp.concatenate([weights[:SIDE], weights[SIDE + OWN :]], axis=0).astype(BF16)
            ds_rim = jnp.concatenate([ds[:SIDE], ds[SIDE + OWN :]], axis=0)
            remote.append((dot(ds_rim, q_ref[rows, cols], 1, 0), dot(low, grad_out, 1, 0)))
        for i in range(2):
            base = i * SIDE
            for g in range(2):
                mine, other = remote[g][i], remote[1 - g][i]
                piece_ref[g, base : base + 2 * BLOCK, cols] = mine[: 2 * BLOCK].astype(BF16)
                piece_ref[g, base + 2 * BLOCK : base + SIDE, cols] = (mine[2 * BLOCK : SIDE] + other[SIDE:]).astype(BF16)

    @pl.when(parity == 0)
    def _():
        far_out[...] = piece_ref[0]
        near_out[...] = piece_ref[1]

    @pl.when(parity == 1)
    def _():
        far_out[...] = piece_ref[1]
        near_out[...] = piece_ref[0]


def spread_matrix(rows, kinds):
    parts = []
    for first, factor, weight, count in kinds:
        row = lax.broadcasted_iota(jnp.int32, (rows, count), 0)
        at = lax.broadcasted_iota(jnp.int32, (rows, count), 1)
        parts.append((((row - first) // factor == at) & (row >= first)).astype(F32) * weight)
    return jnp.concatenate(parts, axis=1).astype(BF16)


def own_kernel(
    where_ref, q_ref, k_ref, mid_ref, far_ref, near_ref, gain_ref, w_ref, att_ref, sums_ref, others_ref, ds_ref, dout_ref,
    normed_ref, dq_ref, own_ref, side_ref,
):
    place_sides(where_ref[0] % 2, far_ref, near_ref, side_ref)
    factor, _ = row_factors(sums_ref, others_ref)
    rows_all = q_ref.shape[0]
    spread = spread_matrix(rows_all, [(0, 4, 0.5, rows_all // 4)])
    for h in range(8):
        cols = slice(h * HDIM, (h + 1) * HDIM)
        inner = []
        for g in range(2):
            rows = slice(g * GROUP, (g + 1) * GROUP)
            normed_ref[rows, cols] = (gain_ref[:, cols] * att_ref[rows, cols] * factor[rows]).astype(BF16)
            ds = ds_ref[g, h]
            keys = window(0, g, cols, side_ref, k_ref, mid_ref)
            dq_ref[rows, cols] = dot(ds, keys, 0, 0).astype(BF16)
            low = w_ref[g, h, SIDE : SIDE + OWN].astype(BF16)
            inner.append((dot(ds[SIDE : SIDE + OWN], q_ref[rows, cols], 1, 0), dot(low, dout_ref[rows, cols], 1, 0)))
        for i in range(2):
            lower, upper = inner[0][i], inner[1][i]
            both_raw = 2 * OWN_RAW - rows_all
            raw = jnp.concatenate(
                [lower[: OWN_RAW - both_raw], lower[OWN_RAW - both_raw : OWN_RAW] + upper[:both_raw], upper[both_raw:OWN_RAW]],
                axis=0,
            )
            low_mid, up_mid = lower[OWN_RAW:], upper[OWN_RAW:]
            both_mid = 2 * OWN_MID - rows_all // 4
            mid = jnp.concatenate(
                [low_mid[: OWN_MID - both_mid], low_mid[OWN_MID - both_mid :] + up_mid[:both_mid], up_mid[both_mid:]], axis=0
            ).astype(BF16)
            own_ref[i, :, cols] = raw + dot(spread, mid, 1, 0)


def final_kernel(where_ref, own_ref, far_ref, near_ref, dk_ref, dv_ref, side_ref):
    place_sides(where_ref[0] % 2, far_ref, near_ref, side_ref)
    rows = own_ref.shape[1]
    spread = [
        spread_matrix(rows, [(rows - BLOCK if g else 0, 1, 1.0, BLOCK), (rows - 4 * BLOCK if g else 0, 4, 0.5, BLOCK), (0, 16, 0.25, BLOCK)])
        for g in range(2)
    ]
    both = jnp.concatenate(spread, axis=1)
    for i, out_ref in enumerate((dk_ref, dv_ref)):
        got = jnp.concatenate([side_ref[0, i * SIDE : (i + 1) * SIDE], side_ref[1, i * SIDE : (i + 1) * SIDE]], axis=0)
        out_ref[...] = (own_ref[i] + dot(both, got, 1, 0)).astype(BF16)


def call(kernel, outs, scratch, flops, args):
    smem = pl.BlockSpec(memory_space=pltpu.SMEM)
    vmem = pl.BlockSpec(memory_space=pltpu.VMEM)
    return pl.pallas_call(
        kernel,
        out_shape=outs,
        in_specs=[smem] + [vmem] * (len(args) - 1),
        out_specs=jax.tree.map(lambda _: vmem, outs),
        scratch_shapes=scratch,
        compiler_params=pltpu.CompilerParams(vmem_limit_bytes=24 * 2**20),
        cost_estimate=pl.CostEstimate(flops=flops, bytes_accessed=4 * 2**20, transcendentals=0),
    )(*args)


def exchange(far, near):
    size = lax.axis_size("seq")
    far_pairs = [(i, i + 1) for i in range(1, size - 1, 2)]
    near_pairs = [(i, i + 1) for i in range(0, size, 2)]
    far_got = lax.ppermute(far, "seq", far_pairs + [(j, i) for i, j in far_pairs])
    near_got = lax.ppermute(near, "seq", near_pairs + [(j, i) for i, j in near_pairs])
    return far_got, near_got


def local(queries, key_vectors, value_vectors, norm_gain, cotangent):
    rows, feats = queries.shape
    index = lax.axis_index("seq").astype(jnp.int32)
    size = lax.axis_size("seq")
    where = jnp.stack([index, (index > 0).astype(jnp.int32), (index < size - 1).astype(jnp.int32)])
    gain = norm_gain.reshape(1, feats)
    heads = feats // HDIM
    arr = jax.ShapeDtypeStruct
    rim = arr((2 * SIDE, feats), BF16)
    sides = pltpu.VMEM((2, 2 * SIDE, feats), BF16)
    far, near, mid = call(
        pack_kernel, (rim, rim, arr((2, rows // 4, feats), BF16)), [], 10**8, (where, key_vectors, value_vectors)
    )
    far, near = exchange(far, near)
    weights, attended, sums = call(
        forward_kernel,
        (arr((2, heads, WINDOW, GROUP), F32), arr((rows, feats), F32), arr((2, rows), F32)),
        [sides, pltpu.VMEM((2, WINDOW, GROUP), F32)],
        10**9,
        (where, queries, key_vectors, value_vectors, mid, far, near, gain, cotangent),
    )
    others = lax.ppermute(sums, "head", [(0, 1), (1, 0)])
    far_piece, near_piece, ds, dout = call(
        pieces_kernel,
        (rim, rim, arr((2, heads, WINDOW, GROUP), BF16), arr((rows, feats), BF16)),
        [sides, sides],
        10**9,
        (where, queries, value_vectors, mid, far, near, gain, cotangent, weights, attended, sums, others),
    )
    far_got, near_got = exchange(far_piece, near_piece)
    normed, query_grad, own = call(
        own_kernel,
        (arr((rows, feats), BF16), arr((rows, feats), BF16), arr((2, rows, feats), F32)),
        [sides],
        10**9,
        (where, queries, key_vectors, mid, far, near, gain, weights, attended, sums, others, ds, dout),
    )
    key_grad, value_grad = call(
        final_kernel, (arr((rows, feats), BF16), arr((rows, feats), BF16)), [sides], 10**8, (where, own, far_got, near_got)
    )
    return normed, query_grad, key_grad, value_grad


def solution(mesh):
    in_specs = (P("seq", "head"), P("seq", "head"), P("seq", "head"), P("head"), P("seq", "head"))
    out_specs = (P("seq", "head"), P("seq", "head"), P("seq", "head"), P("seq", "head"))
    return jax.shard_map(local, mesh=mesh, in_specs=in_specs, out_specs=out_specs, check_vma=False)
```

time: 117 us -> 49 us (0.42)
  starting transfers between devices: 49.5 us -> 24.3 us
  other arithmetic: 18.8 us -> 0.08 us
  matrix products: 11.1 us -> 0 us
  Pallas kernels: 0 us -> 10.6 us
  local copies, waits for them, and re-layouts: 13.6 us -> 4.88 us
  blocking collectives: 7.89 us -> 0 us
  waiting for transfers between devices: 13.8 us -> 7.99 us
    ppermute x12 -> x5, starting transfers between devices: 49.5 us -> 24.3 us  [the longest x2 16.6 us: exchange(): lax.ppermute(far, 'seq', far_pairs + [(j, i) for i, j in far_pairs])]
    dot_general x6 -> x0, matrix products: 11.1 us -> none  [the longest x3 6.41 us: attend(): jnp.einsum('qhd,khd->hqk', query_heads, key_heads, precision=lax.Precisio...]
    pallas_call x0 -> x5, Pallas kernels: none -> 10.6 us  [call(): pl.pallas_call(kernel, out_shape=outs, in_specs=[smem] + [vmem] * (len(ar...]
    reduce_sum x7 -> x0, other arithmetic: 9.83 us -> none  [the longest x2 3.13 us: pool_rows(): jnp.sum(shaped, axis=2, dtype=jnp.float32) * weight]
    psum x1 -> x0, blocking collectives: 7.89 us -> none  [local(): lax.psum((jnp.sum(attended * attended, axis=1), jnp.sum(scaled * attended...]
    ppermute x12 -> x5, waiting for transfers between devices: 13.8 us -> 7.99 us  [the longest x1 4.38 us: local(): others = lax.ppermute(sums, 'head', [(0, 1), (1, 0)])]
    reshape x2 -> x0, local copies, waits for them, and re-layouts: 3.11 us -> none  [attend(): return mixed_heads.reshape(queries.shape[0], head_count * HDIM)]
    sub x1 -> x0, other arithmetic: 2.49 us -> none  [local(): factor[:, None] * scaled]
  transfers between devices with their start and end apart: 12 -> 5, of which waited for: 3 -> 2; matrix products, arithmetic and copies ran while one was open for 9% -> 0% of each run, Pallas kernels for 0% -> 7%
where the time goes in v1:
time: 49 us; the launch traced here: 48.6 us
  starting transfers between devices  24.3 us (50%)
  Pallas kernels  10.6 us (22%)
  waiting for transfers between devices  7.99 us (16%)
  local copies, waits for them, and re-layouts  4.88 us (10%)
  between operations  0.74 us (2%)
    ppermute x2, starting transfers between devices, exchange(): lax.ppermute(far, 'seq', far_pairs + [(j, i) for i, j in far_pairs])  16.6 us
    pallas_call x5, Pallas kernels, call(): pl.pallas_call(kernel, out_shape=outs, in_specs=[smem] + [vmem] * (len(ar...  10.6 us
    unnamed x20, local copies, waits for them, and re-layouts  4.88 us
    ppermute x1, waiting for transfers between devices, local(): others = lax.ppermute(sums, 'head', [(0, 1), (1, 0)])  4.38 us
    ppermute x1, starting transfers between devices, local(): others = lax.ppermute(sums, 'head', [(0, 1), (1, 0)])  3.85 us
    ppermute x2, starting transfers between devices, exchange(): lax.ppermute(near, 'seq', near_pairs + [(j, i) for i, j in near_pairs])  3.84 us
    ppermute x2, waiting for transfers between devices, exchange(): lax.ppermute(far, 'seq', far_pairs + [(j, i) for i, j in far_pairs])  3.61 us
  transfers between devices with their start and end apart: 5, of which 2 were waited for; matrix products, arithmetic and copies ran while one was open for 0% of the time, Pallas kernels for 7%

profile of v1, /device:TPU:255, one launch (start us, length us, event | category | flops | bytes accessed | tf_op | source)
XLA Modules:
  0.0 48.6 jit_solution(18288453867483753139)
XLA Ops:
  0.6 0.1 pad_add_fusion.where_ref
  0.7 1.0 %copy-done = bf16[256,1024]{1,0:T(8,128)(2,1)S(1)} copy-done((bf16[256,1024]{1,0:T(8,128)(2,1)S(1)}, bf16[256,1024]{1,0:T(8,128)(2,1)}, u32[]{:S(2)}) %copy-start) | copy-done | bytes 524312
  1.8 1.0 %copy-done.4 = bf16[256,1024]{1,0:T(8,128)(2,1)S(1)} copy-done((bf16[256,1024]{1,0:T(8,128)(2,1)S(1)}, bf16[256,1024]{1,0:T(8,128)(2,1)}, u32[]{:S(2)}) %copy-start.4) | copy-done | bytes 524312
  2.8 0.8 %shard_map.84 = (bf16[96,1024]{1,0:T(8,128)(2,1)S(1)}, bf16[96,1024]{1,0:T(8,128)(2,1)S(1)}, bf16[2,64,1024]{2,1,0:T(8,128)(2,1)S(1)}) custom-call(s32[3]{0:T(128)S(1)} %pad_add_fusion.where_ref, bf16[256,1024]{1,0:T(8,128)(2,1)S(1)} %copy-done, bf16[256,1024]{1,0:T(8,128)(2,1)S(1)} %copy-done.4), custom_call_target="tpu_custom_call" | custom-call | flops 100000000 | bytes 4194304 | tf_op jit(solution)/shard_map/pallas_call | solution.py:242
  3.7 8.0 %collective-permute-start = (bf16[96,1024]{1,0:T(8,128)(2,1)S(1)}, bf16[96,1024]{1,0:T(8,128)(2,1)S(1)}, u32[]{:S(2)}, u32[]{:S(2)}) collective-permute-start(bf16[96,1024]{1,0:T(8,128)(2,1)S(1)} %get-tuple-element.20), channel_id=1, source_target_pairs={{2,4},{6,8},{10,12},{14,16},{18,20},{22,24},{26,28},{30,32},{34,36... | collective-permute-start | bytes 589832 | tf_op jit(solution)/shard_map/ppermute | solution.py:257
  11.7 1.9 %collective-permute-start.1 = (bf16[96,1024]{1,0:T(8,128)(2,1)S(1)}, bf16[96,1024]{1,0:T(8,128)(2,1)S(1)}, u32[]{:S(2)}, u32[]{:S(2)}) collective-permute-start(bf16[96,1024]{1,0:T(8,128)(2,1)S(1)} %get-tuple-element.21), channel_id=1, source_target_pairs={{0,2},{4,6},{8,10},{12,14},{16,18},{20,22},{24,26},{28,30},{32,34}... | collective-permute-start | bytes 589832 | tf_op jit(solution)/shard_map/ppermute | solution.py:258
  13.6 3.6 %collective-permute-done.far_ref = bf16[96,1024]{1,0:T(8,128)(2,1)S(1)} collective-permute-done((bf16[96,1024]{1,0:T(8,128)(2,1)S(1)}, bf16[96,1024]{1,0:T(8,128)(2,1)S(1)}, u32[]{:S(2)}, u32[]{:S(2)}) %collective-permute-start) | collective-permute-done | bytes 196640 | tf_op jit(solution)/shard_map/ppermute | solution.py:257
  17.2 0.0 collective-permute-done.1.near_ref
  17.2 1.0 %copy-done.2 = bf16[256,1024]{1,0:T(8,128)(2,1)S(1)} copy-done((bf16[256,1024]{1,0:T(8,128)(2,1)S(1)}, bf16[256,1024]{1,0:T(8,128)(2,1)}, u32[]{:S(2)}) %copy-start.2) | copy-done | bytes 524312
  18.3 1.0 %copy-done.6 = bf16[256,1024]{1,0:T(8,128)(2,1)S(1)} copy-done((bf16[256,1024]{1,0:T(8,128)(2,1)S(1)}, bf16[256,1024]{1,0:T(8,128)(2,1)}, u32[]{:S(2)}) %copy-start.6) | copy-done | bytes 524312
  19.3 0.7 %copy-done.8 = f32[1024]{0:T(1024)S(1)} copy-done((f32[1024]{0:T(1024)S(1)}, f32[1024]{0:T(1024)}, u32[]{:S(2)}) %copy-start.8) | copy-done | bytes 4120
  20.0 2.4 %shard_map.85 = (f32[2,8,256,128]{3,2,1,0:T(8,128)S(1)}, f32[256,1024]{1,0:T(8,128)S(1)}, f32[2,256]{1,0:T(2,128)S(1)}) custom-call(s32[3]{0:T(128)S(1)} %pad_add_fusion.where_ref, bf16[256,1024]{1,0:T(8,128)(2,1)S(1)} %copy-done.2, bf16[256,1024]{1,0:T(8,128)(2,1)S(1)} %copy-done, bf16[256,1024]{1,0:T(8,128)(2,1)S(1)} %copy-done.4, ...), custom_call_target="tpu_custom_call" | custom-call | flops 1000000000 | bytes 4194304 | tf_op jit(solution)/shard_map/pallas_call | solution.py:242
  22.4 3.9 %collective-permute-start.2 = (f32[2,256]{1,0:T(2,128)S(1)}, f32[2,256]{1,0:T(2,128)S(1)}, u32[]{:S(2)}, u32[]{:S(2)}) collective-permute-start(f32[2,256]{1,0:T(2,128)S(1)} %get-tuple-element.24.sums_ref), channel_id=1, source_target_pairs={{0,1},{1,0},{2,3},{3,2},{4,5},{5,4},{6,7},{7,6},{8,9},{9,8},{10,11... | collective-permute-start | bytes 6152 | tf_op jit(solution)/shard_map/ppermute | solution.py:283
  26.3 4.4 %collective-permute-done.2.others_ref = f32[2,256]{1,0:T(2,128)S(1)} collective-permute-done((f32[2,256]{1,0:T(2,128)S(1)}, f32[2,256]{1,0:T(2,128)S(1)}, u32[]{:S(2)}, u32[]{:S(2)}) %collective-permute-start.2) | collective-permute-done | bytes 2080 | tf_op jit(solution)/shard_map/ppermute | solution.py:283
  30.6 0.0 copy-done.3
  30.6 0.0 copy-start.1
  30.7 0.0 copy-start.9
  30.7 1.9 %shard_map.86 = (bf16[96,1024]{1,0:T(8,128)(2,1)S(1)}, bf16[96,1024]{1,0:T(8,128)(2,1)S(1)}, bf16[2,8,256,128]{3,2,1,0:T(8,128)(2,1)S(1)}, bf16[256,1024]{1,0:T(8,128)(2,1)S(1)}) custom-call(s32[3]{0:T(128)S(1)} %pad_add_fusion.where_ref, bf16[256,1024]{1,0:T(8,128)(2,1)S(1)} %copy-done.3, bf16[256,1024]{1,0:T(8,128)(2,1)S(1)} %copy-done.5, ...), custom_call_target="tpu_custom_call" | custom-call | flops 1000000000 | bytes 4194304 | tf_op jit(solution)/shard_map/pallas_call | solution.py:242
  32.6 8.6 %collective-permute-start.3 = (bf16[96,1024]{1,0:T(8,128)(2,1)S(1)}, bf16[96,1024]{1,0:T(8,128)(2,1)S(1)}, u32[]{:S(2)}, u32[]{:S(2)}) collective-permute-start(bf16[96,1024]{1,0:T(8,128)(2,1)S(1)} %get-tuple-element.30), channel_id=1, source_target_pairs={{2,4},{6,8},{10,12},{14,16},{18,20},{22,24},{26,28},{30,32},{34,36... | collective-permute-start | bytes 589832 | tf_op jit(solution)/shard_map/ppermute | solution.py:257
  41.2 1.9 %collective-permute-start.4 = (bf16[96,1024]{1,0:T(8,128)(2,1)S(1)}, bf16[96,1024]{1,0:T(8,128)(2,1)S(1)}, u32[]{:S(2)}, u32[]{:S(2)}) collective-permute-start(bf16[96,1024]{1,0:T(8,128)(2,1)S(1)} %get-tuple-element.31), channel_id=1, source_target_pairs={{0,2},{4,6},{8,10},{12,14},{16,18},{20,22},{24,26},{28,30},{32,34}... | collective-permute-start | bytes 589832 | tf_op jit(solution)/shard_map/ppermute | solution.py:258
  43.2 3.5 %shard_map.87 = (bf16[256,1024]{1,0:T(8,128)(2,1)}, bf16[256,1024]{1,0:T(8,128)(2,1)}, f32[2,256,1024]{2,1,0:T(8,128)S(1)}) custom-call(s32[3]{0:T(128)S(1)} %pad_add_fusion.where_ref, bf16[256,1024]{1,0:T(8,128)(2,1)S(1)} %copy-done.3, bf16[256,1024]{1,0:T(8,128)(2,1)S(1)} %copy-done.1, bf16[2,64,1024]{2,1,0:T(8,128)(2,1)S(1)} %get-tuple-element.19.mid_ref, ...), custom_call_target="tpu_custom_call" | custom-call | flops 1000000000 | bytes 4194304 | tf_op jit(solution)/shard_map/pallas_call | solution.py:242
  46.6 0.0 collective-permute-done.3.far_ref
  46.6 0.0 collective-permute-done.4.near_ref
  46.6 2.0 %shard_map.88 = (bf16[256,1024]{1,0:T(8,128)(2,1)}, bf16[256,1024]{1,0:T(8,128)(2,1)}) custom-call(s32[3]{0:T(128)S(1)} %pad_add_fusion.where_ref, f32[2,256,1024]{2,1,0:T(8,128)S(1)} %get-tuple-element.29.own_ref, bf16[96,1024]{1,0:T(8,128)(2,1)S(1)} %collective-permute-done.3.far_ref, bf16[96,1024]{1,0:T(8,128)(2,1)S(1)} %collective-permute-done.4.near_ref), custom_call_target="tpu_custom_call" | custom-call | flops 100000000 | bytes 4194304 | tf_op jit(solution)/shard_map/pallas_call | solution.py:242
  (12 shorter events, 0.0 us)
Async XLA Ops:
  0.7 1.0 %copy-start = (bf16[256,1024]{1,0:T(8,128)(2,1)S(1)}, bf16[256,1024]{1,0:T(8,128)(2,1)}, u32[]{:S(2)}) copy-start(bf16[256,1024]{1,0:T(8,128)(2,1)} %k_ref.5) | copy-start | bytes 1572868
  1.8 1.0 %copy-start.4 = (bf16[256,1024]{1,0:T(8,128)(2,1)S(1)}, bf16[256,1024]{1,0:T(8,128)(2,1)}, u32[]{:S(2)}) copy-start(bf16[256,1024]{1,0:T(8,128)(2,1)} %v_ref.5) | copy-start | bytes 1572868
  2.8 27.8 %copy-start.3 = (bf16[256,1024]{1,0:T(8,128)(2,1)S(1)}, bf16[256,1024]{1,0:T(8,128)(2,1)}, u32[]{:S(2)}) copy-start(bf16[256,1024]{1,0:T(8,128)(2,1)} %q_ref.5) | copy-start | bytes 1572868
  2.8 27.8 %copy-start.5 = (bf16[256,1024]{1,0:T(8,128)(2,1)S(1)}, bf16[256,1024]{1,0:T(8,128)(2,1)}, u32[]{:S(2)}) copy-start(bf16[256,1024]{1,0:T(8,128)(2,1)} %v_ref.5) | copy-start | bytes 1572868
  3.7 13.6 %collective-permute-start = (bf16[96,1024]{1,0:T(8,128)(2,1)S(1)}, bf16[96,1024]{1,0:T(8,128)(2,1)S(1)}, u32[]{:S(2)}, u32[]{:S(2)}) collective-permute-start(bf16[96,1024]{1,0:T(8,128)(2,1)S(1)} %get-tuple-element.20), channel_id=1, source_target_pairs={{2,4},{6,8},{10,12},{14,16},{18,20},{22,24},{26,28},{30,32},{34,36... | collective-permute-start | bytes 589832 | tf_op jit(solution)/shard_map/ppermute | solution.py:257
  11.7 5.5 %collective-permute-start.1 = (bf16[96,1024]{1,0:T(8,128)(2,1)S(1)}, bf16[96,1024]{1,0:T(8,128)(2,1)S(1)}, u32[]{:S(2)}, u32[]{:S(2)}) collective-permute-start(bf16[96,1024]{1,0:T(8,128)(2,1)S(1)} %get-tuple-element.21), channel_id=1, source_target_pairs={{0,2},{4,6},{8,10},{12,14},{16,18},{20,22},{24,26},{28,30},{32,34}... | collective-permute-start | bytes 589832 | tf_op jit(solution)/shard_map/ppermute | solution.py:258
  17.2 1.0 %copy-start.2 = (bf16[256,1024]{1,0:T(8,128)(2,1)S(1)}, bf16[256,1024]{1,0:T(8,128)(2,1)}, u32[]{:S(2)}) copy-start(bf16[256,1024]{1,0:T(8,128)(2,1)} %q_ref.5) | copy-start | bytes 1572868
  18.3 1.0 %copy-start.6 = (bf16[256,1024]{1,0:T(8,128)(2,1)S(1)}, bf16[256,1024]{1,0:T(8,128)(2,1)}, u32[]{:S(2)}) copy-start(bf16[256,1024]{1,0:T(8,128)(2,1)} %cot_ref.3) | copy-start | bytes 1572868
  19.3 0.7 %copy-start.8 = (f32[1024]{0:T(1024)S(1)}, f32[1024]{0:T(1024)}, u32[]{:S(2)}) copy-start(f32[1024]{0:T(1024)} %param.8) | copy-start | bytes 12292
  20.0 10.6 %copy-start.7 = (bf16[256,1024]{1,0:T(8,128)(2,1)S(1)}, bf16[256,1024]{1,0:T(8,128)(2,1)}, u32[]{:S(2)}) copy-start(bf16[256,1024]{1,0:T(8,128)(2,1)} %cot_ref.3) | copy-start | bytes 1572868
  22.4 8.2 %collective-permute-start.2 = (f32[2,256]{1,0:T(2,128)S(1)}, f32[2,256]{1,0:T(2,128)S(1)}, u32[]{:S(2)}, u32[]{:S(2)}) collective-permute-start(f32[2,256]{1,0:T(2,128)S(1)} %get-tuple-element.24.sums_ref), channel_id=1, source_target_pairs={{0,1},{1,0},{2,3},{3,2},{4,5},{5,4},{6,7},{7,6},{8,9},{9,8},{10,11... | collective-permute-start | bytes 6152 | tf_op jit(solution)/shard_map/ppermute | solution.py:283
  30.6 12.5 %copy-start.1 = (bf16[256,1024]{1,0:T(8,128)(2,1)S(1)}, bf16[256,1024]{1,0:T(8,128)(2,1)}, u32[]{:S(2)}) copy-start(bf16[256,1024]{1,0:T(8,128)(2,1)} %k_ref.5) | copy-start | bytes 1572868
  30.7 12.5 %copy-start.9 = (f32[1024]{0:T(1024)S(1)}, f32[1024]{0:T(1024)}, u32[]{:S(2)}) copy-start(f32[1024]{0:T(1024)} %param.8) | copy-start | bytes 12292
  32.6 14.0 %collective-permute-start.3 = (bf16[96,1024]{1,0:T(8,128)(2,1)S(1)}, bf16[96,1024]{1,0:T(8,128)(2,1)S(1)}, u32[]{:S(2)}, u32[]{:S(2)}) collective-permute-start(bf16[96,1024]{1,0:T(8,128)(2,1)S(1)} %get-tuple-element.30), channel_id=1, source_target_pairs={{2,4},{6,8},{10,12},{14,16},{18,20},{22,24},{26,28},{30,32},{34,36... | collective-permute-start | bytes 589832 | tf_op jit(solution)/shard_map/ppermute | solution.py:257
  41.2 5.4 %collective-permute-start.4 = (bf16[96,1024]{1,0:T(8,128)(2,1)S(1)}, bf16[96,1024]{1,0:T(8,128)(2,1)S(1)}, u32[]{:S(2)}, u32[]{:S(2)}) collective-permute-start(bf16[96,1024]{1,0:T(8,128)(2,1)S(1)} %get-tuple-element.31), channel_id=1, source_target_pairs={{0,2},{4,6},{8,10},{12,14},{16,18},{20,22},{24,26},{28,30},{32,34}... | collective-permute-start | bytes 589832 | tf_op jit(solution)/shard_map/ppermute | solution.py:258

commit v2 on v1

v2 whole, which is shorter than its diff:
```python
from functools import partial

import jax
import jax.numpy as jnp
from jax import lax
from jax.experimental import pallas as pl
from jax.experimental.pallas import tpu as pltpu
from jax.sharding import PartitionSpec as P

HEADS = 16
HDIM = 128
BLOCK = 16
SCALE = HDIM**-0.5
F32 = jnp.float32
BF16 = jnp.bfloat16

SIDE = 3 * BLOCK
OWN_RAW = 9 * BLOCK
OWN_MID = 3 * BLOCK
OWN = OWN_RAW + OWN_MID
WINDOW = SIDE + OWN + BLOCK
GROUP = 128


def dot(a, b, ca, cb):
    return lax.dot_general(a, b, (((ca,), (cb,)), ((), ())), preferred_element_type=F32)


def pool_matrix(rows):
    shape = (rows // 4 + rows // 16, rows)
    out_row = lax.broadcasted_iota(jnp.int32, shape, 0)
    row = lax.broadcasted_iota(jnp.int32, shape, 1)
    middle = (row // 4 == out_row).astype(F32) * 0.5
    coarse = (row // 16 == out_row - rows // 4).astype(F32) * 0.25
    return jnp.where(out_row < rows // 4, middle, coarse).astype(BF16)


def pack_side(i, k_or_v, upper, mid_ref, coarse_ref, out_ref):
    raw_at = pl.multiple_of(upper * (k_or_v.shape[0] - BLOCK), BLOCK)
    mid_at = pl.multiple_of(upper * (mid_ref.shape[1] - BLOCK), BLOCK)
    base = i * SIDE
    out_ref[base : base + BLOCK] = k_or_v[pl.ds(raw_at, BLOCK)]
    out_ref[base + BLOCK : base + 2 * BLOCK] = mid_ref[i, pl.ds(mid_at, BLOCK)]
    out_ref[base + 2 * BLOCK : base + 3 * BLOCK] = coarse_ref[i]


def pack_kernel(
    where_ref, k_hbm, v_hbm, q_hbm, cot_hbm, gain_hbm,
    k_ref, v_ref, q_ref, cot_ref, gain_ref, far_ref, mid_ref, coarse_ref, sems,
):
    copies = [
        pltpu.make_async_copy(src, dst, sems.at[n])
        for n, (src, dst) in enumerate(
            [(k_hbm, k_ref), (v_hbm, v_ref), (q_hbm, q_ref), (cot_hbm, cot_ref), (gain_hbm, gain_ref)]
        )
    ]
    for copy in copies:
        copy.start()
    rows = k_ref.shape[0]
    mids = rows // 4
    upper = where_ref[0] % 2
    pool = pool_matrix(rows)
    for i, ref in enumerate((k_ref, v_ref)):
        copies[i].wait()
        pooled = dot(pool, ref[...], 1, 0).astype(BF16)
        mid_ref[i] = pooled[:mids]
        coarse_ref[i] = pooled[mids:]
        pack_side(i, ref, upper, mid_ref, coarse_ref, far_ref)
    for copy in copies[2:]:
        copy.wait()


def place_sides(parity, far_ref, near_ref, side_ref):
    @pl.when(parity == 0)
    def _():
        side_ref[0] = far_ref[...]
        side_ref[1] = near_ref[...]

    @pl.when(parity == 1)
    def _():
        side_ref[0] = near_ref[...]
        side_ref[1] = far_ref[...]


def own_rows(i, g, cols, raw_ref, mid_ref):
    raw_at, mid_at = (g * (raw_ref.shape[0] - OWN_RAW), g * (mid_ref.shape[1] - OWN_MID))
    return [raw_ref[raw_at : raw_at + OWN_RAW, cols], mid_ref[i, mid_at : mid_at + OWN_MID, cols]]


def side_rows(i, g, cols, side_ref):
    base = i * SIDE
    return [side_ref[g, base : base + SIDE, cols], side_ref[1 - g, base + 2 * BLOCK : base + SIDE, cols]]


def window(i, g, cols, side_ref, raw_ref, mid_ref):
    mine, other = side_rows(i, g, cols, side_ref)
    return jnp.concatenate([mine, *own_rows(i, g, cols, raw_ref, mid_ref), other], axis=0)


def allowed(g, has_below, has_above):
    shape = (WINDOW, GROUP)
    kb = lax.broadcasted_iota(jnp.int32, shape, 0) // BLOCK
    qb = lax.broadcasted_iota(jnp.int32, shape, 1) // BLOCK
    qm = qb // 4
    raw_gap = kb - 3 - g - qb
    mid_gap = kb - 12 - g - qm
    edge_raw = qb == (7 if g else 0)
    edge_mid = qm == (1 if g else 0)
    one = jnp.ones(shape, jnp.int32)
    none = jnp.zeros(shape, jnp.int32)
    own = jnp.where(kb < 12, jnp.where(jnp.abs(raw_gap) <= 1, one, none), jnp.where(jnp.abs(mid_gap) == 1, one, none))
    side = jnp.where(kb == 0, jnp.where(edge_raw, one, none), jnp.where(kb == 1, jnp.where(edge_mid, one, none), one))
    valid_side, valid_other = (has_above, has_below) if g else (has_below, has_above)
    return jnp.where(kb < 3, side * valid_side, jnp.where(kb == 15, one * valid_other, own))


def local_kernel(
    where_ref, q_ref, k_ref, v_ref, mid_ref, coarse_ref, near_ref, lifted_ref, stats_ref, bias_ref
):
    for i, ref in enumerate((k_ref, v_ref)):
        pack_side(i, ref, 1 - where_ref[0] % 2, mid_ref, coarse_ref, near_ref)
    heads = lifted_ref.shape[1]
    for g in range(2):
        bias_ref[...] = jnp.where(allowed(g, 1, 1)[SIDE : SIDE + OWN] == 1, 0.0, -1e30)
        rows = slice(g * GROUP, (g + 1) * GROUP)
        for h in range(heads):
            cols = slice(h * HDIM, (h + 1) * HDIM)
            keys = jnp.concatenate(own_rows(0, g, cols, k_ref, mid_ref), axis=0)
            scores = dot(keys, q_ref[rows, cols], 1, 1) * SCALE + bias_ref[...]
            highest = jnp.max(scores, axis=0, keepdims=True)
            lifted = jnp.exp(scores - highest)
            lifted_ref[g, h] = lifted
            stats_ref[g, h : h + 1] = highest
            stats_ref[g, heads + h : heads + h + 1] = jnp.sum(lifted, axis=0, keepdims=True)


def forward_kernel(
    where_ref, q_ref, v_ref, mid_ref, far_ref, near_ref, gain_ref, cot_ref, lifted_ref, stats_ref,
    w_ref, att_ref, sums_ref, side_ref, bias_ref, side_lifted, side_stats,
):
    place_sides(where_ref[0] % 2, far_ref, near_ref, side_ref)
    heads = lifted_ref.shape[1]
    for g in range(2):
        ok = allowed(g, where_ref[1], where_ref[2])
        bias_ref[g] = jnp.where(jnp.concatenate([ok[:SIDE], ok[SIDE + OWN :]], axis=0) == 1, 0.0, -1e30)
    for g in range(2):
        rows = slice(g * GROUP, (g + 1) * GROUP)
        for h in range(heads):
            cols = slice(h * HDIM, (h + 1) * HDIM)
            keys = jnp.concatenate(side_rows(0, g, cols, side_ref), axis=0)
            scores = dot(keys, q_ref[rows, cols], 1, 1) * SCALE + bias_ref[g]
            highest = jnp.max(scores, axis=0, keepdims=True)
            lifted = jnp.exp(scores - highest)
            side_lifted[g, h] = lifted
            side_stats[g, h : h + 1] = highest
            side_stats[g, heads + h : heads + h + 1] = jnp.sum(lifted, axis=0, keepdims=True)
    for g in range(2):
        rows = slice(g * GROUP, (g + 1) * GROUP)
        own_high, side_high = stats_ref[g, :heads], side_stats[g, :heads]
        highest = jnp.maximum(own_high, side_high)
        own_part, side_part = jnp.exp(own_high - highest), jnp.exp(side_high - highest)
        inverse = 1.0 / (stats_ref[g, heads:] * own_part + side_stats[g, heads:] * side_part)
        own_part, side_part = own_part * inverse, side_part * inverse
        squares = jnp.zeros((GROUP, HDIM), F32)
        crossed = jnp.zeros((GROUP, HDIM), F32)
        for h in range(heads):
            cols = slice(h * HDIM, (h + 1) * HDIM)
            side_w = side_lifted[g, h] * side_part[h : h + 1]
            own_w = lifted_ref[g, h] * own_part[h : h + 1]
            weights = jnp.concatenate([side_w[:SIDE], own_w, side_w[SIDE:]], axis=0)
            w_ref[g, h] = weights
            mixed = dot(weights.astype(BF16), window(1, g, cols, side_ref, v_ref, mid_ref), 0, 0)
            att_ref[rows, cols] = mixed
            squares += mixed * mixed
            crossed += mixed * (cot_ref[rows, cols].astype(F32) * gain_ref[:, cols])
        sums_ref[0:1, rows] = jnp.sum(squares.T, axis=0, keepdims=True)
        sums_ref[1:2, rows] = jnp.sum(crossed.T, axis=0, keepdims=True)


def row_factors(sums_ref):
    feat_all = HEADS * HDIM
    totals = sums_ref[0] + sums_ref[1]
    factor = lax.rsqrt(totals[0:1] / feat_all + 1e-06)
    cross = factor * factor * factor * totals[1:2] / feat_all
    both = jnp.concatenate([factor, cross, jnp.zeros((6, factor.shape[1]), F32)], axis=0)
    columns = both.T
    return columns[:, 0:1], columns[:, 1:2]


def side_piece(g, q_ref, w_ref, ds_ref, dout_ref, out_ref):
    half = q_ref.shape[0] // 2
    mine = pl.ds(pl.multiple_of(g * half, half), half)
    other = pl.ds(pl.multiple_of((1 - g) * half, half), half)
    blank = jnp.zeros((2 * BLOCK, GROUP), BF16)
    for h in range(w_ref.shape[1]):
        cols = slice(h * HDIM, (h + 1) * HDIM)
        for i, (left, right) in enumerate(((ds_ref, q_ref), (w_ref, dout_ref))):
            far_part = jnp.concatenate([blank, left[1 - g, h, SIDE + OWN :].astype(BF16)], axis=0)
            lhs = jnp.concatenate([left[g, h, :SIDE].astype(BF16), far_part], axis=1)
            rhs = jnp.concatenate([right[mine, cols], right[other, cols]], axis=0)
            out_ref[i * SIDE : (i + 1) * SIDE, cols] = dot(lhs, rhs, 1, 0).astype(BF16)


def pieces_kernel(
    where_ref, q_ref, v_ref, mid_ref, side_ref, gain_ref, cot_ref, w_ref, att_ref, sums_ref,
    far_out, near_out, ds_ref, dout_ref,
):
    factor, cross = row_factors(sums_ref)
    for h in range(w_ref.shape[1]):
        cols = slice(h * HDIM, (h + 1) * HDIM)
        for g in range(2):
            rows = slice(g * GROUP, (g + 1) * GROUP)
            scaled = cot_ref[rows, cols].astype(F32) * gain_ref[:, cols]
            grad_out = (factor[rows] * scaled - cross[rows] * att_ref[rows, cols]).astype(BF16)
            dout_ref[rows, cols] = grad_out
            grad_w = dot(window(1, g, cols, side_ref, v_ref, mid_ref), grad_out, 1, 1)
            weights = w_ref[g, h]
            middle = jnp.sum(weights * grad_w, axis=0, keepdims=True)
            ds_ref[g, h] = (weights * (grad_w - middle) * SCALE).astype(BF16)
    side_piece(where_ref[0] % 2, q_ref, w_ref, ds_ref, dout_ref, far_out)
    side_piece(1 - where_ref[0] % 2, q_ref, w_ref, ds_ref, dout_ref, near_out)


def spread_matrix(rows, kinds):
    parts = []
    for first, factor, weight, count in kinds:
        row = lax.broadcasted_iota(jnp.int32, (rows, count), 0)
        at = lax.broadcasted_iota(jnp.int32, (rows, count), 1)
        parts.append((((row - first) // factor == at) & (row >= first)).astype(F32) * weight)
    return jnp.concatenate(parts, axis=1).astype(BF16)


def own_kernel(
    where_ref, q_ref, k_ref, mid_ref, side_ref, gain_ref, w_ref, att_ref, sums_ref, ds_ref, dout_ref,
    own_ref, normed_hbm, dq_hbm, normed_ref, dq_ref, sems,
):
    rows_all, feats = q_ref.shape
    factor, _ = row_factors(sums_ref)
    normed_ref[...] = (gain_ref[...] * att_ref[...] * factor).astype(BF16)
    copies = [pltpu.make_async_copy(normed_ref, normed_hbm, sems.at[0])]
    copies[0].start()
    spread = spread_matrix(rows_all, [(0, 4, 0.5, rows_all // 4)])
    heads = w_ref.shape[1]
    for h in range(heads):
        cols = slice(h * HDIM, (h + 1) * HDIM)
        inner = []
        for g in range(2):
            rows = slice(g * GROUP, (g + 1) * GROUP)
            ds = ds_ref[g, h]
            keys = window(0, g, cols, side_ref, k_ref, mid_ref)
            dq_ref[rows, cols] = dot(ds, keys, 0, 0).astype(BF16)
            low = w_ref[g, h, SIDE : SIDE + OWN].astype(BF16)
            inner.append((dot(ds[SIDE : SIDE + OWN], q_ref[rows, cols], 1, 0), dot(low, dout_ref[rows, cols], 1, 0)))
        if h % (heads // 2) == heads // 2 - 1:
            done = pl.ds((h + 1 - heads // 2) * HDIM, heads // 2 * HDIM)
            copies.append(pltpu.make_async_copy(dq_ref.at[:, done], dq_hbm.at[:, done], sems.at[len(copies)]))
            copies[-1].start()
        for i in range(2):
            lower, upper = inner[0][i], inner[1][i]
            both_raw = 2 * OWN_RAW - rows_all
            raw = jnp.concatenate(
                [lower[: OWN_RAW - both_raw], lower[OWN_RAW - both_raw : OWN_RAW] + upper[:both_raw], upper[both_raw:OWN_RAW]],
                axis=0,
            )
            low_mid, up_mid = lower[OWN_RAW:], upper[OWN_RAW:]
            both_mid = 2 * OWN_MID - rows_all // 4
            mid = jnp.concatenate(
                [low_mid[: OWN_MID - both_mid], low_mid[OWN_MID - both_mid :] + up_mid[:both_mid], up_mid[both_mid:]], axis=0
            ).astype(BF16)
            own_ref[i, :, cols] = raw + dot(spread, mid, 1, 0)
    for copy in copies:
        copy.wait()


def final_kernel(where_ref, own_ref, far_ref, near_ref, dk_hbm, dv_hbm, dk_ref, dv_ref, side_ref, sems):
    place_sides(where_ref[0] % 2, far_ref, near_ref, side_ref)
    rows = own_ref.shape[1]
    spread = [
        spread_matrix(rows, [(rows - BLOCK if g else 0, 1, 1.0, BLOCK), (rows - 4 * BLOCK if g else 0, 4, 0.5, BLOCK), (0, 16, 0.25, BLOCK)])
        for g in range(2)
    ]
    both = jnp.concatenate(spread, axis=1)
    copies = []
    for i, (out_ref, hbm) in enumerate(((dk_ref, dk_hbm), (dv_ref, dv_hbm))):
        got = jnp.concatenate([side_ref[0, i * SIDE : (i + 1) * SIDE], side_ref[1, i * SIDE : (i + 1) * SIDE]], axis=0)
        for part in range(2):
            at = slice(part * (rows // 2), (part + 1) * (rows // 2))
            out_ref[at] = (own_ref[i, at] + dot(both[at], got, 1, 0)).astype(BF16)
            copies.append(pltpu.make_async_copy(out_ref.at[at], hbm.at[at], sems.at[len(copies)]))
            copies[-1].start()
    for copy in copies:
        copy.wait()


SMEM = pl.BlockSpec(memory_space=pltpu.SMEM)
VMEM = pl.BlockSpec(memory_space=pltpu.VMEM)
HBM = pl.BlockSpec(memory_space=pltpu.HBM)


def call(kernel, args, in_specs, outs, out_specs, scratch, flops):
    return pl.pallas_call(
        kernel,
        out_shape=outs,
        in_specs=[SMEM, *in_specs],
        out_specs=out_specs,
        scratch_shapes=scratch,
        compiler_params=pltpu.CompilerParams(vmem_limit_bytes=24 * 2**20),
        cost_estimate=pl.CostEstimate(flops=flops, bytes_accessed=4 * 2**20, transcendentals=0),
    )(*args)


def far_swap(x):
    pairs = [(i, i + 1) for i in range(1, lax.axis_size("seq") - 1, 2)]
    return lax.ppermute(x, "seq", pairs + [(j, i) for i, j in pairs])


def near_swap(x):
    pairs = [(i, i + 1) for i in range(0, lax.axis_size("seq"), 2)]
    return lax.ppermute(x, "seq", pairs + [(j, i) for i, j in pairs])


def local(queries, key_vectors, value_vectors, norm_gain, cotangent):
    rows, feats = queries.shape
    index = lax.axis_index("seq").astype(jnp.int32)
    size = lax.axis_size("seq")
    where = jnp.stack([index, (index > 0).astype(jnp.int32), (index < size - 1).astype(jnp.int32)])
    heads = feats // HDIM
    inputs = (key_vectors, value_vectors, queries, cotangent, norm_gain.reshape(1, feats))
    arr = jax.ShapeDtypeStruct
    dma = pltpu.SemaphoreType.DMA
    whole = arr((rows, feats), BF16)
    rim = arr((2 * SIDE, feats), BF16)
    k, v, q, cot, gain, far, mid, coarse = call(
        pack_kernel,
        (where, *(pltpu.with_memory_space_constraint(x, pltpu.HBM) for x in inputs)),
        [HBM] * 5,
        (whole, whole, whole, whole, arr((1, feats), F32), rim, arr((2, rows // 4, feats), BF16), arr((2, BLOCK, feats), BF16)),
        (VMEM,) * 8,
        [dma((5,))],
        10**8,
    )
    far_got = far_swap(far)
    near, lifted, stats = call(
        local_kernel,
        (where, q, k, v, mid, coarse),
        [VMEM] * 5,
        (rim, arr((2, heads, OWN, GROUP), F32), arr((2, 2 * heads, GROUP), F32)),
        (VMEM,) * 3,
        [pltpu.VMEM((OWN, GROUP), F32)],
        10**9,
    )
    near_got = near_swap(near)
    weights, attended, sums, side = call(
        forward_kernel,
        (where, q, v, mid, far_got, near_got, gain, cot, lifted, stats),
        [VMEM] * 9,
        (arr((2, heads, WINDOW, GROUP), F32), arr((rows, feats), F32), arr((2, rows), F32), arr((2, 2 * SIDE, feats), BF16)),
        (VMEM,) * 4,
        [
            pltpu.VMEM((2, SIDE + BLOCK, GROUP), F32),
            pltpu.VMEM((2, heads, SIDE + BLOCK, GROUP), F32),
            pltpu.VMEM((2, 2 * heads, GROUP), F32),
        ],
        10**9,
    )
    sums = lax.all_gather(sums, "head")
    far_piece, near_piece, ds, dout = call(
        pieces_kernel,
        (where, q, v, mid, side, gain, cot, weights, attended, sums),
        [VMEM] * 9,
        (rim, rim, arr((2, heads, WINDOW, GROUP), BF16), whole),
        (VMEM,) * 4,
        [],
        10**9,
    )
    far_back = far_swap(far_piece)
    near_back = near_swap(near_piece)
    own, normed, query_grad = call(
        own_kernel,
        (where, q, k, mid, side, gain, weights, attended, sums, ds, dout),
        [VMEM] * 10,
        (arr((2, rows, feats), F32), whole, whole),
        (VMEM, HBM, HBM),
        [pltpu.VMEM((rows, feats), BF16), pltpu.VMEM((rows, feats), BF16), dma((3,))],
        10**9,
    )
    key_grad, value_grad = call(
        final_kernel,
        (where, own, far_back, near_back),
        [VMEM] * 3,
        (whole, whole),
        (HBM, HBM),
        [pltpu.VMEM((rows, feats), BF16), pltpu.VMEM((rows, feats), BF16), pltpu.VMEM((2, 2 * SIDE, feats), BF16), dma((4,))],
        10**8,
    )
    return normed, query_grad, key_grad, value_grad


def solution(mesh):
    in_specs = (P("seq", "head"), P("seq", "head"), P("seq", "head"), P("head"), P("seq", "head"))
    out_specs = (P("seq", "head"), P("seq", "head"), P("seq", "head"), P("seq", "head"))
    return jax.shard_map(local, mesh=mesh, in_specs=in_specs, out_specs=out_specs, check_vma=False)
```

time: 49 us -> 43.5 us (0.89)
  blocking collectives: 0 us -> 7.1 us
  waiting for transfers between devices: 7.99 us -> 2.34 us
  local copies, waits for them, and re-layouts: 4.88 us -> 0 us
  starting transfers between devices: 24.3 us -> 20.5 us
  Pallas kernels: 10.6 us -> 12.6 us
    all_gather x0 -> x1, blocking collectives: none -> 7.1 us  [local(): sums = lax.all_gather(sums, 'head')]
    ppermute x5 -> x4, waiting for transfers between devices: 7.99 us -> 2.34 us  [the longest x2 2.34 us: far_swap(): return lax.ppermute(x, 'seq', pairs + [(j, i) for i, j in pairs])]
    unnamed x20 -> x0, local copies, waits for them, and re-layouts: 4.88 us -> none
    ppermute x5 -> x4, starting transfers between devices: 24.3 us -> 20.5 us  [the longest x2 16.7 us: far_swap(): return lax.ppermute(x, 'seq', pairs + [(j, i) for i, j in pairs])]
    pallas_call x5 -> x6, Pallas kernels: 10.6 us -> 12.6 us  [call(): pl.pallas_call(kernel, out_shape=outs, in_specs=[SMEM, *in_specs], out_sp...]
  transfers between devices with their start and end apart: 5 -> 4, of which waited for: 2 -> 1; matrix products, arithmetic and copies ran while one was open for 0% -> 0% of each run, Pallas kernels for 7% -> 10%
where the time goes in v2:
time: 43.5 us; the launch traced here: 43.3 us
  starting transfers between devices  20.5 us (47%)
  Pallas kernels  12.6 us (29%)
  blocking collectives  7.1 us (16%)
  waiting for transfers between devices  2.34 us (5%)
  between operations  0.72 us (2%)
    ppermute x2, starting transfers between devices, far_swap(): return lax.ppermute(x, 'seq', pairs + [(j, i) for i, j in pairs])  16.7 us
    pallas_call x6, Pallas kernels, call(): pl.pallas_call(kernel, out_shape=outs, in_specs=[SMEM, *in_specs], out_sp...  12.6 us
    all_gather x1, blocking collectives, local(): sums = lax.all_gather(sums, 'head')  7.1 us
    ppermute x2, starting transfers between devices, near_swap(): return lax.ppermute(x, 'seq', pairs + [(j, i) for i, j in pairs])  3.84 us
    ppermute x2, waiting for transfers between devices, far_swap(): return lax.ppermute(x, 'seq', pairs + [(j, i) for i, j in pairs])  2.34 us
  transfers between devices with their start and end apart: 4, of which 1 were waited for; matrix products, arithmetic and copies ran while one was open for 0% of the time, Pallas kernels for 10%

profile of v2, /device:TPU:255, one launch (start us, length us, event | category | flops | bytes accessed | tf_op | source)
XLA Modules:
  0.0 43.3 jit_solution(16421093758374690709)
XLA Ops:
  0.6 0.1 pad_add_fusion.where_ref
  0.7 2.1 %shard_map.84 = (bf16[256,1024]{1,0:T(8,128)(2,1)S(1)}, bf16[256,1024]{1,0:T(8,128)(2,1)S(1)}, bf16[256,1024]{1,0:T(8,128)(2,1)S(1)}, bf16[256,1024]{1,0:T(8,128...) custom-call(s32[3]{0:T(128)S(1)} %pad_add_fusion.where_ref, ...), custom_call_target="tpu_custom_call" | custom-call | flops 100000000 | bytes 4194304 | tf_op jit(solution)/shard_map/pallas_call | solution.py:301
  2.8 8.0 %collective-permute-start = (bf16[96,1024]{1,0:T(8,128)(2,1)S(1)}, bf16[96,1024]{1,0:T(8,128)(2,1)S(1)}, u32[]{:S(2)}, u32[]{:S(2)}) collective-permute-start(bf16[96,1024]{1,0:T(8,128)(2,1)S(1)} %get-tuple-element.32), channel_id=1, source_target_pairs={{2,4},{6,8},{10,12},{14,16},{18,20},{22,24},{26,28},{30,32},{34,36... | collective-permute-start | bytes 589832 | tf_op jit(solution)/shard_map/ppermute | solution.py:314
  10.9 1.3 %shard_map.85 = (bf16[96,1024]{1,0:T(8,128)(2,1)S(1)}, f32[2,8,192,128]{3,2,1,0:T(8,128)S(1)}, f32[2,16,128]{2,1,0:T(8,128)S(1)}) custom-call(s32[3]{0:T(128)S(1)} %pad_add_fusion.where_ref, bf16[256,1024]{1,0:T(8,128)(2,1)S(1)} %get-tuple-element.28.q_ref, bf16[256,1024]{1,0:T(8,128)(2,1)S(1)} %get-tuple-element.29.k_ref, ...), custom_call_target="tpu_custom_call" | custom-call | flops 1000000000 | bytes 4194304 | tf_op jit(solution)/shard_map/pallas_call | solution.py:301
  12.2 1.9 %collective-permute-start.1 = (bf16[96,1024]{1,0:T(8,128)(2,1)S(1)}, bf16[96,1024]{1,0:T(8,128)(2,1)S(1)}, u32[]{:S(2)}, u32[]{:S(2)}) collective-permute-start(bf16[96,1024]{1,0:T(8,128)(2,1)S(1)} %get-tuple-element.34), channel_id=1, source_target_pairs={{0,2},{4,6},{8,10},{12,14},{16,18},{20,22},{24,26},{28,30},{32,34}... | collective-permute-start | bytes 589832 | tf_op jit(solution)/shard_map/ppermute | solution.py:319
  14.1 2.3 %collective-permute-done.far_ref = bf16[96,1024]{1,0:T(8,128)(2,1)S(1)} collective-permute-done((bf16[96,1024]{1,0:T(8,128)(2,1)S(1)}, bf16[96,1024]{1,0:T(8,128)(2,1)S(1)}, u32[]{:S(2)}, u32[]{:S(2)}) %collective-permute-start) | collective-permute-done | bytes 196640 | tf_op jit(solution)/shard_map/ppermute | solution.py:314
  16.4 0.0 collective-permute-done.1.near_ref
  16.4 1.7 %shard_map.86 = (f32[2,8,256,128]{3,2,1,0:T(8,128)S(1)}, f32[256,1024]{1,0:T(8,128)S(1)}, f32[2,256]{1,0:T(2,128)S(1)}, bf16[2,96,1024]{2,1,0:T(8,128)(2,1)S(1)}) custom-call(s32[3]{0:T(128)S(1)} %pad_add_fusion.where_ref, bf16[256,1024]{1,0:T(8,128)(2,1)S(1)} %get-tuple-element.28.q_ref, bf16[256,1024]{1,0:T(8,128)(2,1)S(1)} %get-tuple-element.31.v_ref, ...), custom_call_target="tpu_custom_call" | custom-call | flops 1000000000 | bytes 4194304 | tf_op jit(solution)/shard_map/pallas_call | solution.py:301
  18.1 7.1 %all-gather.1.sums_ref = f32[2,2,256]{2,1,0:T(2,128)S(1)} all-gather(f32[1,2,256]{2,1,0:T(2,128)S(1)} %bitcast.5), channel_id=2, replica_groups=mesh['seq'=256,'head'=2] {'head'}, dimensions={0}, use_global_device_ids=true | all-gather | bytes 6144 | tf_op jit(solution)/shard_map/all_gather | solution.py:366
  25.2 2.3 %shard_map.87 = (bf16[96,1024]{1,0:T(8,128)(2,1)S(1)}, bf16[96,1024]{1,0:T(8,128)(2,1)S(1)}, bf16[2,8,256,128]{3,2,1,0:T(8,128)(2,1)S(1)}, bf16[256,1024]{1,0:T(8,128)(2,1)S(1)}) custom-call(s32[3]{0:T(128)S(1)} %pad_add_fusion.where_ref, bf16[256,1024]{1,0:T(8,128)(2,1)S(1)} %get-tuple-element.28.q_ref, bf16[256,1024]{1,0:T(8,128)(2,1)S(1)} %get-tuple-element.31.v_ref, ...), custom_call_target="tpu_custom_call" | custom-call | flops 1000000000 | bytes 4194304 | tf_op jit(solution)/shard_map/pallas_call | solution.py:301
  27.5 8.6 %collective-permute-start.2 = (bf16[96,1024]{1,0:T(8,128)(2,1)S(1)}, bf16[96,1024]{1,0:T(8,128)(2,1)S(1)}, u32[]{:S(2)}, u32[]{:S(2)}) collective-permute-start(bf16[96,1024]{1,0:T(8,128)(2,1)S(1)} %get-tuple-element.48), channel_id=1, source_target_pairs={{2,4},{6,8},{10,12},{14,16},{18,20},{22,24},{26,28},{30,32},{34,36... | collective-permute-start | bytes 589832 | tf_op jit(solution)/shard_map/ppermute | solution.py:314
  36.1 1.9 %collective-permute-start.3 = (bf16[96,1024]{1,0:T(8,128)(2,1)S(1)}, bf16[96,1024]{1,0:T(8,128)(2,1)S(1)}, u32[]{:S(2)}, u32[]{:S(2)}) collective-permute-start(bf16[96,1024]{1,0:T(8,128)(2,1)S(1)} %get-tuple-element.49), channel_id=1, source_target_pairs={{0,2},{4,6},{8,10},{12,14},{16,18},{20,22},{24,26},{28,30},{32,34}... | collective-permute-start | bytes 589832 | tf_op jit(solution)/shard_map/ppermute | solution.py:319
  38.1 3.2 %shard_map.88 = (f32[2,256,1024]{2,1,0:T(8,128)S(1)}, bf16[256,1024]{1,0:T(8,128)(2,1)}, bf16[256,1024]{1,0:T(8,128)(2,1)}) custom-call(s32[3]{0:T(128)S(1)} %pad_add_fusion.where_ref, bf16[256,1024]{1,0:T(8,128)(2,1)S(1)} %get-tuple-element.28.q_ref, bf16[256,1024]{1,0:T(8,128)(2,1)S(1)} %get-tuple-element.29.k_ref, ...), custom_call_target="tpu_custom_call" | custom-call | flops 1000000000 | bytes 4194304 | tf_op jit(solution)/shard_map/pallas_call | solution.py:301
  41.3 0.0 collective-permute-done.2.far_ref
  41.3 0.0 collective-permute-done.3.near_ref
  41.3 2.0 %shard_map.89 = (bf16[256,1024]{1,0:T(8,128)(2,1)}, bf16[256,1024]{1,0:T(8,128)(2,1)}) custom-call(s32[3]{0:T(128)S(1)} %pad_add_fusion.where_ref, f32[2,256,1024]{2,1,0:T(8,128)S(1)} %get-tuple-element.47.own_ref, bf16[96,1024]{1,0:T(8,128)(2,1)S(1)} %collective-permute-done.2.far_ref, bf16[96,1024]{1,0:T(8,128)(2,1)S(1)} %collective-permute-done.3.near_ref), custom_call_target="tpu_custom_call" | custom-call | flops 100000000 | bytes 4194304 | tf_op jit(solution)/shard_map/pallas_call | solution.py:301
Async XLA Ops:
  2.8 13.6 %collective-permute-start = (bf16[96,1024]{1,0:T(8,128)(2,1)S(1)}, bf16[96,1024]{1,0:T(8,128)(2,1)S(1)}, u32[]{:S(2)}, u32[]{:S(2)}) collective-permute-start(bf16[96,1024]{1,0:T(8,128)(2,1)S(1)} %get-tuple-element.32), channel_id=1, source_target_pairs={{2,4},{6,8},{10,12},{14,16},{18,20},{22,24},{26,28},{30,32},{34,36... | collective-permute-start | bytes 589832 | tf_op jit(solution)/shard_map/ppermute | solution.py:314
  12.2 4.3 %collective-permute-start.1 = (bf16[96,1024]{1,0:T(8,128)(2,1)S(1)}, bf16[96,1024]{1,0:T(8,128)(2,1)S(1)}, u32[]{:S(2)}, u32[]{:S(2)}) collective-permute-start(bf16[96,1024]{1,0:T(8,128)(2,1)S(1)} %get-tuple-element.34), channel_id=1, source_target_pairs={{0,2},{4,6},{8,10},{12,14},{16,18},{20,22},{24,26},{28,30},{32,34}... | collective-permute-start | bytes 589832 | tf_op jit(solution)/shard_map/ppermute | solution.py:319
  27.5 13.8 %collective-permute-start.2 = (bf16[96,1024]{1,0:T(8,128)(2,1)S(1)}, bf16[96,1024]{1,0:T(8,128)(2,1)S(1)}, u32[]{:S(2)}, u32[]{:S(2)}) collective-permute-start(bf16[96,1024]{1,0:T(8,128)(2,1)S(1)} %get-tuple-element.48), channel_id=1, source_target_pairs={{2,4},{6,8},{10,12},{14,16},{18,20},{22,24},{26,28},{30,32},{34,36... | collective-permute-start | bytes 589832 | tf_op jit(solution)/shard_map/ppermute | solution.py:314
  36.1 5.2 %collective-permute-start.3 = (bf16[96,1024]{1,0:T(8,128)(2,1)S(1)}, bf16[96,1024]{1,0:T(8,128)(2,1)S(1)}, u32[]{:S(2)}, u32[]{:S(2)}) collective-permute-start(bf16[96,1024]{1,0:T(8,128)(2,1)S(1)} %get-tuple-element.49), channel_id=1, source_target_pairs={{0,2},{4,6},{8,10},{12,14},{16,18},{20,22},{24,26},{28,30},{32,34}... | collective-permute-start | bytes 589832 | tf_op jit(solution)/shard_map/ppermute | solution.py:319

commit v3 on v2

v3 whole, which is shorter than its diff:
```python
from functools import partial

import jax
import jax.numpy as jnp
from jax import lax
from jax.experimental import pallas as pl
from jax.experimental.pallas import tpu as pltpu
from jax.sharding import PartitionSpec as P

HEADS = 16
HDIM = 128
BLOCK = 16
SCALE = HDIM**-0.5
F32 = jnp.float32
BF16 = jnp.bfloat16

SIDE = 3 * BLOCK
RIM = SIDE + BLOCK
OWN_RAW = 9 * BLOCK
OWN_MID = 3 * BLOCK
OWN = OWN_RAW + OWN_MID
WINDOW = RIM + OWN
GROUP = 128


def dot(a, b, ca, cb):
    return lax.dot_general(a, b, (((ca,), (cb,)), ((), ())), preferred_element_type=F32)


def parity():
    return lax.axis_index("seq") % 2


def has_sides():
    index = lax.axis_index("seq")
    return (index > 0).astype(jnp.int32), (index < lax.axis_size("seq") - 1).astype(jnp.int32)


def pool_matrix(rows):
    shape = (rows // 4 + rows // 16, rows)
    out_row = lax.broadcasted_iota(jnp.int32, shape, 0)
    row = lax.broadcasted_iota(jnp.int32, shape, 1)
    middle = (row // 4 == out_row).astype(F32) * 0.5
    coarse = (row // 16 == out_row - rows // 4).astype(F32) * 0.25
    return jnp.where(out_row < rows // 4, middle, coarse).astype(BF16)


def pack_side(i, k_or_v, upper, mid_ref, coarse_ref, out_ref):
    raw_at = pl.multiple_of(upper * (k_or_v.shape[0] - BLOCK), BLOCK)
    mid_at = pl.multiple_of(upper * (mid_ref.shape[1] - BLOCK), BLOCK)
    base = i * SIDE
    out_ref[base : base + BLOCK] = k_or_v[pl.ds(raw_at, BLOCK)]
    out_ref[base + BLOCK : base + 2 * BLOCK] = mid_ref[i, pl.ds(mid_at, BLOCK)]
    out_ref[base + 2 * BLOCK : base + 3 * BLOCK] = coarse_ref[i]


def pack_kernel(k_hbm, v_hbm, k_ref, v_ref, far_ref, near_ref, mid_ref, coarse_ref, sems):
    copies = [pltpu.make_async_copy(k_hbm, k_ref, sems.at[0]), pltpu.make_async_copy(v_hbm, v_ref, sems.at[1])]
    for copy in copies:
        copy.start()
    rows = k_ref.shape[0]
    mids = rows // 4
    upper = parity()
    pool = pool_matrix(rows)
    for i, ref in enumerate((k_ref, v_ref)):
        copies[i].wait()
        pooled = dot(pool, ref[...], 1, 0).astype(BF16)
        mid_ref[i] = pooled[:mids]
        coarse_ref[i] = pooled[mids:]
        pack_side(i, ref, upper, mid_ref, coarse_ref, far_ref)
        pack_side(i, ref, 1 - upper, mid_ref, coarse_ref, near_ref)


def place_sides(odd, far_ref, near_ref, side_ref):
    @pl.when(odd == 0)
    def _():
        side_ref[0] = far_ref[...]
        side_ref[1] = near_ref[...]

    @pl.when(odd == 1)
    def _():
        side_ref[0] = near_ref[...]
        side_ref[1] = far_ref[...]


def own_rows(i, g, cols, raw_ref, mid_ref):
    raw_at, mid_at = (g * (raw_ref.shape[0] - OWN_RAW), g * (mid_ref.shape[1] - OWN_MID))
    return [raw_ref[raw_at : raw_at + OWN_RAW, cols], mid_ref[i, mid_at : mid_at + OWN_MID, cols]]


def side_rows(i, g, cols, side_ref):
    base = i * SIDE
    return [side_ref[g, base : base + SIDE, cols], side_ref[1 - g, base + 2 * BLOCK : base + SIDE, cols]]


def window(i, g, cols, side_ref, raw_ref, mid_ref):
    return jnp.concatenate([*side_rows(i, g, cols, side_ref), *own_rows(i, g, cols, raw_ref, mid_ref)], axis=0)


def allowed(g, has_below, has_above):
    shape = (WINDOW, GROUP)
    kb = lax.broadcasted_iota(jnp.int32, shape, 0) // BLOCK
    qb = lax.broadcasted_iota(jnp.int32, shape, 1) // BLOCK
    qm = qb // 4
    raw_gap = kb - 4 - g - qb
    mid_gap = kb - 13 - g - qm
    edge_raw = qb == (7 if g else 0)
    edge_mid = qm == (1 if g else 0)
    one = jnp.ones(shape, jnp.int32)
    none = jnp.zeros(shape, jnp.int32)
    own = jnp.where(kb < 13, jnp.where(jnp.abs(raw_gap) <= 1, one, none), jnp.where(jnp.abs(mid_gap) == 1, one, none))
    side = jnp.where(kb == 0, jnp.where(edge_raw, one, none), jnp.where(kb == 1, jnp.where(edge_mid, one, none), one))
    valid_side, valid_other = (has_above, has_below) if g else (has_below, has_above)
    return jnp.where(kb < 3, side * valid_side, jnp.where(kb == 3, one * valid_other, own))


def local_kernel(
    k_ref, v_ref, mid_ref, q_hbm, cot_hbm, gain_hbm,
    q_ref, gain_ref, scaled_ref, lifted_ref, stats_ref, mix_ref, bias_ref, cot_ref, own_bias, sems,
):
    copies = [
        pltpu.make_async_copy(src, dst, sems.at[n])
        for n, (src, dst) in enumerate([(q_hbm, q_ref), (cot_hbm, cot_ref), (gain_hbm, gain_ref)])
    ]
    for copy in copies:
        copy.start()
    for g in range(2):
        bias = jnp.where(allowed(g, *has_sides()) == 1, 0.0, -1e30)
        bias_ref[g] = bias[:RIM]
        own_bias[g] = bias[RIM:]
    for copy in copies:
        copy.wait()
    heads = lifted_ref.shape[1]
    for g in range(2):
        rows = slice(g * GROUP, (g + 1) * GROUP)
        for h in range(heads):
            cols = slice(h * HDIM, (h + 1) * HDIM)
            keys = jnp.concatenate(own_rows(0, g, cols, k_ref, mid_ref), axis=0)
            scores = dot(keys, q_ref[rows, cols], 1, 1) * SCALE + own_bias[g]
            highest = jnp.max(scores, axis=0, keepdims=True)
            lifted = jnp.exp(scores - highest)
            lifted_ref[g, h] = lifted
            stats_ref[g, h : h + 1] = highest
            stats_ref[g, heads + h : heads + h + 1] = jnp.sum(lifted, axis=0, keepdims=True)
            scaled_ref[g, h] = (cot_ref[rows, cols].astype(F32) * gain_ref[:, cols]).T
    for g in range(2):
        for h in range(heads):
            values = jnp.concatenate(own_rows(1, g, slice(h * HDIM, (h + 1) * HDIM), v_ref, mid_ref), axis=0)
            mix_ref[g, h] = dot(values, lifted_ref[g, h].astype(BF16), 0, 0)


def forward_kernel(
    q_ref, far_ref, near_ref, bias_ref, scaled_ref, stats_ref, mix_ref,
    side_ref, side_w, own_scale, att_ref, sums_ref, side_stats,
):
    place_sides(parity(), far_ref, near_ref, side_ref)
    heads = mix_ref.shape[1]
    for g in range(2):
        rows = slice(g * GROUP, (g + 1) * GROUP)
        for h in range(heads):
            cols = slice(h * HDIM, (h + 1) * HDIM)
            keys = jnp.concatenate(side_rows(0, g, cols, side_ref), axis=0)
            scores = dot(keys, q_ref[rows, cols], 1, 1) * SCALE + bias_ref[g]
            highest = jnp.max(scores, axis=0, keepdims=True)
            lifted = jnp.exp(scores - highest)
            side_w[g, h] = lifted
            side_stats[g, h : h + 1] = highest
            side_stats[g, heads + h : heads + h + 1] = jnp.sum(lifted, axis=0, keepdims=True)
    for g in range(2):
        rows = slice(g * GROUP, (g + 1) * GROUP)
        own_high, side_high = stats_ref[g, :heads], side_stats[g, :heads]
        highest = jnp.maximum(own_high, side_high)
        own_part, side_part = jnp.exp(own_high - highest), jnp.exp(side_high - highest)
        inverse = 1.0 / (stats_ref[g, heads:] * own_part + side_stats[g, heads:] * side_part)
        own_part, side_part = own_part * inverse, side_part * inverse
        own_scale[g] = own_part
        squares = jnp.zeros((HDIM, GROUP), F32)
        crossed = jnp.zeros((HDIM, GROUP), F32)
        for h in range(heads):
            cols = slice(h * HDIM, (h + 1) * HDIM)
            weights = side_w[g, h] * side_part[h : h + 1]
            side_w[g, h] = weights
            values = jnp.concatenate(side_rows(1, g, cols, side_ref), axis=0)
            mixed = mix_ref[g, h] * own_part[h : h + 1] + dot(values, weights.astype(BF16), 0, 0)
            att_ref[g, h] = mixed
            squares += mixed * mixed
            crossed += mixed * scaled_ref[g, h]
        sums_ref[0:1, rows] = jnp.sum(squares, axis=0, keepdims=True)
        sums_ref[1:2, rows] = jnp.sum(crossed, axis=0, keepdims=True)


def row_factors(sums_ref):
    feat_all = HEADS * HDIM
    totals = sums_ref[0] + sums_ref[1]
    factor = lax.rsqrt(totals[0:1] / feat_all + 1e-06)
    return factor, factor * factor * factor * totals[1:2] / feat_all


def side_piece(g, q_ref, side_w, ds_ref, dout_ref, out_ref):
    half = q_ref.shape[0] // 2
    mine = pl.ds(pl.multiple_of(g * half, half), half)
    other = pl.ds(pl.multiple_of((1 - g) * half, half), half)
    blank = jnp.zeros((2 * BLOCK, GROUP), BF16)
    for h in range(side_w.shape[1]):
        cols = slice(h * HDIM, (h + 1) * HDIM)
        lefts = [
            jnp.concatenate(
                [ref[g, h, :SIDE].astype(BF16), jnp.concatenate([blank, ref[1 - g, h, SIDE:RIM].astype(BF16)], axis=0)], axis=1
            )
            for ref in (ds_ref, side_w)
        ]
        queries = jnp.concatenate([q_ref[mine, cols], q_ref[other, cols]], axis=0)
        out_ref[:SIDE, cols] = dot(lefts[0], queries, 1, 0).astype(BF16)
        douts = jnp.concatenate([dout_ref[g, h], dout_ref[1 - g, h]], axis=1)
        out_ref[SIDE:, cols] = dot(lefts[1], douts, 1, 1).astype(BF16)


def pieces_kernel(
    q_ref, v_ref, mid_ref, side_ref, scaled_ref, lifted_ref, side_w, own_scale, att_ref, sums_ref,
    far_out, near_out, ds_ref, dout_ref,
):
    factor, cross = row_factors(sums_ref)
    for h in range(side_w.shape[1]):
        cols = slice(h * HDIM, (h + 1) * HDIM)
        for g in range(2):
            rows = slice(g * GROUP, (g + 1) * GROUP)
            grad_out = (factor[:, rows] * scaled_ref[g, h] - cross[:, rows] * att_ref[g, h]).astype(BF16)
            dout_ref[g, h] = grad_out
            grad_w = dot(window(1, g, cols, side_ref, v_ref, mid_ref), grad_out, 1, 0)
            weights = jnp.concatenate([side_w[g, h], lifted_ref[g, h] * own_scale[g, h : h + 1]], axis=0)
            middle = jnp.sum(weights * grad_w, axis=0, keepdims=True)
            ds_ref[g, h] = (weights * (grad_w - middle) * SCALE).astype(BF16)
    upper = parity()
    side_piece(upper, q_ref, side_w, ds_ref, dout_ref, far_out)
    side_piece(1 - upper, q_ref, side_w, ds_ref, dout_ref, near_out)


def spread_matrix(rows, kinds):
    parts = []
    for first, factor, weight, count in kinds:
        row = lax.broadcasted_iota(jnp.int32, (rows, count), 0)
        at = lax.broadcasted_iota(jnp.int32, (rows, count), 1)
        parts.append((((row - first) // factor == at) & (row >= first)).astype(F32) * weight)
    return jnp.concatenate(parts, axis=1).astype(BF16)


def own_kernel(
    q_ref, k_ref, mid_ref, side_ref, gain_ref, lifted_ref, own_scale, att_ref, sums_ref, ds_ref, dout_ref,
    own_ref, spread_ref, normed_hbm, dq_hbm, normed_ref, dq_ref, mid_grad, sems,
):
    rows_all = q_ref.shape[0]
    heads = lifted_ref.shape[1]
    factor, _ = row_factors(sums_ref)
    copies = []
    spread = spread_matrix(rows_all, [(0, 4, 0.5, rows_all // 4)])
    for h in range(heads):
        cols = slice(h * HDIM, (h + 1) * HDIM)
        inner = []
        for g in range(2):
            rows = slice(g * GROUP, (g + 1) * GROUP)
            normed_ref[rows, cols] = ((att_ref[g, h] * factor[:, rows]).T * gain_ref[:, cols]).astype(BF16)
            ds = ds_ref[g, h]
            keys = window(0, g, cols, side_ref, k_ref, mid_ref)
            dq_ref[rows, cols] = dot(ds, keys, 0, 0).astype(BF16)
            low = (lifted_ref[g, h] * own_scale[g, h : h + 1]).astype(BF16)
            inner.append((dot(ds[RIM:], q_ref[rows, cols], 1, 0), dot(low, dout_ref[g, h], 1, 1)))
        if h % (heads // 2) == heads // 2 - 1:
            done = pl.ds((h + 1 - heads // 2) * HDIM, heads // 2 * HDIM)
            for ref, hbm in ((normed_ref, normed_hbm), (dq_ref, dq_hbm)):
                copies.append(pltpu.make_async_copy(ref.at[:, done], hbm.at[:, done], sems.at[len(copies)]))
                copies[-1].start()
        for i in range(2):
            lower, upper = inner[0][i], inner[1][i]
            both_raw = 2 * OWN_RAW - rows_all
            raw = jnp.concatenate(
                [lower[: OWN_RAW - both_raw], lower[OWN_RAW - both_raw : OWN_RAW] + upper[:both_raw], upper[both_raw:OWN_RAW]],
                axis=0,
            )
            own_ref[i, :, cols] = raw
            low_mid, up_mid = lower[OWN_RAW:], upper[OWN_RAW:]
            both_mid = 2 * OWN_MID - rows_all // 4
            mid_grad[i, :, cols] = jnp.concatenate(
                [low_mid[: OWN_MID - both_mid], low_mid[OWN_MID - both_mid :] + up_mid[:both_mid], up_mid[both_mid:]], axis=0
            ).astype(BF16)
    for i in range(2):
        own_ref[i] += dot(spread, mid_grad[i], 1, 0)
    for g in range(2):
        raw_at, mid_at = (rows_all - BLOCK, rows_all - 4 * BLOCK) if g else (0, 0)
        spread_ref[g] = spread_matrix(rows_all, [(raw_at, 1, 1.0, BLOCK), (mid_at, 4, 0.5, BLOCK), (0, 16, 0.25, BLOCK)])
    for copy in copies:
        copy.wait()


def final_kernel(own_ref, spread_ref, far_ref, near_ref, dk_hbm, dv_hbm, dk_ref, dv_ref, sems):
    rows = own_ref.shape[1]
    upper = parity()
    both = jnp.concatenate([spread_ref[upper], spread_ref[1 - upper]], axis=1)
    copies = []
    for i, (out_ref, hbm) in enumerate(((dk_ref, dk_hbm), (dv_ref, dv_hbm))):
        got = jnp.concatenate([far_ref[i * SIDE : (i + 1) * SIDE], near_ref[i * SIDE : (i + 1) * SIDE]], axis=0)
        for part in range(2):
            at = slice(part * (rows // 2), (part + 1) * (rows // 2))
            out_ref[at] = (own_ref[i, at] + dot(both[at], got, 1, 0)).astype(BF16)
            copies.append(pltpu.make_async_copy(out_ref.at[at], hbm.at[at], sems.at[len(copies)]))
            copies[-1].start()
    for copy in copies:
        copy.wait()


VMEM = pl.BlockSpec(memory_space=pltpu.VMEM)
HBM = pl.BlockSpec(memory_space=pltpu.HBM)


def call(kernel, args, outs, scratch, flops):
    placed = [pltpu.with_memory_space_constraint(x, pltpu.HBM) if space is HBM else x for x, space in args]
    return pl.pallas_call(
        kernel,
        out_shape=tuple(shape for shape, _ in outs),
        in_specs=[space for _, space in args],
        out_specs=tuple(space for _, space in outs),
        scratch_shapes=scratch,
        compiler_params=pltpu.CompilerParams(vmem_limit_bytes=24 * 2**20),
        cost_estimate=pl.CostEstimate(flops=flops, bytes_accessed=4 * 2**20, transcendentals=0),
    )(*placed)


def on(space, *xs):
    return [(x, space) for x in xs]


def far_swap(x):
    pairs = [(i, i + 1) for i in range(1, lax.axis_size("seq") - 1, 2)]
    return lax.ppermute(x, "seq", pairs + [(j, i) for i, j in pairs])


def near_swap(x):
    pairs = [(i, i + 1) for i in range(0, lax.axis_size("seq"), 2)]
    return lax.ppermute(x, "seq", pairs + [(j, i) for i, j in pairs])


def local(queries, key_vectors, value_vectors, norm_gain, cotangent):
    rows, feats = queries.shape
    heads = feats // HDIM
    gain = norm_gain.reshape(1, feats)
    arr = jax.ShapeDtypeStruct
    dma = pltpu.SemaphoreType.DMA
    whole = arr((rows, feats), BF16)
    rim = arr((2 * SIDE, feats), BF16)
    tiles = arr((2, heads, HDIM, GROUP), F32)
    k, v, far, near, mid = call(
        pack_kernel,
        on(HBM, key_vectors, value_vectors),
        on(VMEM, whole, whole, rim, rim, arr((2, rows // 4, feats), BF16)),
        [pltpu.VMEM((2, BLOCK, feats), BF16), dma((2,))],
        10**8,
    )
    far_got = far_swap(far)
    near_got = near_swap(near)
    q, gain, scaled, lifted, stats, mix, bias = call(
        local_kernel,
        on(VMEM, k, v, mid) + on(HBM, queries, cotangent, gain),
        on(
            VMEM, whole, arr((1, feats), F32), tiles, arr((2, heads, OWN, GROUP), F32), arr((2, 2 * heads, GROUP), F32),
            tiles, arr((2, RIM, GROUP), F32),
        ),
        [pltpu.VMEM((rows, feats), BF16), pltpu.VMEM((2, OWN, GROUP), F32), dma((3,))],
        10**9,
    )
    side, side_w, own_scale, attended, sums = call(
        forward_kernel,
        on(VMEM, q, far_got, near_got, bias, scaled, stats, mix),
        on(
            VMEM, arr((2, 2 * SIDE, feats), BF16), arr((2, heads, RIM, GROUP), F32), arr((2, heads, GROUP), F32),
            tiles, arr((2, rows), F32),
        ),
        [pltpu.VMEM((2, 2 * heads, GROUP), F32)],
        10**9,
    )
    sums = lax.all_gather(sums, "head")
    far_piece, near_piece, ds, dout = call(
        pieces_kernel,
        on(VMEM, q, v, mid, side, scaled, lifted, side_w, own_scale, attended, sums),
        on(VMEM, rim, rim, arr((2, heads, WINDOW, GROUP), BF16), arr((2, heads, HDIM, GROUP), BF16)),
        [],
        10**9,
    )
    far_back = far_swap(far_piece)
    near_back = near_swap(near_piece)
    own, spread, normed, query_grad = call(
        own_kernel,
        on(VMEM, q, k, mid, side, gain, lifted, own_scale, attended, sums, ds, dout),
        on(VMEM, arr((2, rows, feats), F32), arr((2, rows, SIDE), BF16)) + on(HBM, whole, whole),
        [pltpu.VMEM((rows, feats), BF16), pltpu.VMEM((rows, feats), BF16), pltpu.VMEM((2, rows // 4, feats), BF16), dma((4,))],
        10**9,
    )
    key_grad, value_grad = call(
        final_kernel,
        on(VMEM, own, spread, far_back, near_back),
        on(HBM, whole, whole),
        [pltpu.VMEM((rows, feats), BF16), pltpu.VMEM((rows, feats), BF16), dma((4,))],
        10**8,
    )
    return normed, query_grad, key_grad, value_grad


def solution(mesh):
    in_specs = (P("seq", "head"), P("seq", "head"), P("seq", "head"), P("head"), P("seq", "head"))
    out_specs = (P("seq", "head"), P("seq", "head"), P("seq", "head"), P("seq", "head"))
    return jax.shard_map(local, mesh=mesh, in_specs=in_specs, out_specs=out_specs, check_vma=False)
```

time: 43.5 us -> 40.1 us (0.922)
  the two profiles are of different devices: /device:TPU:255 before, /device:TPU:288 now
where the time goes in v3:
time: 40.1 us; the launch traced here: 39.9 us
  waiting for transfers between devices  11.3 us (28%)
  starting transfers between devices  10.3 us (26%)
  Pallas kernels  9.32 us (23%)
  blocking collectives  8.25 us (21%)
  between operations  0.69 us (2%)
    ppermute x2, waiting for transfers between devices, far_swap(): return lax.ppermute(x, 'seq', pairs + [(j, i) for i, j in pairs])  11.3 us
    pallas_call x6, Pallas kernels, call(): pl.pallas_call(kernel, out_shape=tuple((shape for shape, _ in outs)), in_...  9.32 us
    all_gather x1, blocking collectives, local(): sums = lax.all_gather(sums, 'head')  8.25 us
    ppermute x2, starting transfers between devices, far_swap(): return lax.ppermute(x, 'seq', pairs + [(j, i) for i, j in pairs])  6.5 us
    ppermute x2, starting transfers between devices, near_swap(): return lax.ppermute(x, 'seq', pairs + [(j, i) for i, j in pairs])  3.84 us
  transfers between devices with their start and end apart: 4, of which 2 were waited for; matrix products, arithmetic and copies ran while one was open for 0% of the time, Pallas kernels for 11%

profile of v3, /device:TPU:288, one launch (start us, length us, event | category | flops | bytes accessed | tf_op | source)
XLA Modules:
  0.0 39.9 jit_solution(1050520390874277991)
XLA Ops:
  0.6 1.5 %shard_map.84 = (bf16[256,1024]{1,0:T(8,128)(2,1)S(1)}, bf16[256,1024]{1,0:T(8,128)(2,1)S(1)}, bf16[96,1024]{1,0:T(8,128)(2,1)S(1)}, bf16[96,1024]{1,0:T(8,128)(2,1)S(1)}, bf16[2,64,1024]{2,1,0:T(8,128)(2,1)S(1)}) custom-call(bf16[256,1024]{1,0:T(8,128)(2,1)} %k_hbm.1, bf16[256,1024]{1,0:T(8,128)(2,1)} %v_hbm.1), custom_call_target="tpu_custom_call" | custom-call | flops 100000000 | bytes 4194304 | tf_op jit(solution)/shard_map/pallas_call | solution.py:316
  2.1 3.5 %collective-permute-start = (bf16[96,1024]{1,0:T(8,128)(2,1)S(1)}, bf16[96,1024]{1,0:T(8,128)(2,1)S(1)}, u32[]{:S(2)}, u32[]{:S(2)}) collective-permute-start(bf16[96,1024]{1,0:T(8,128)(2,1)S(1)} %get-tuple-element.35), channel_id=1, source_target_pairs={{2,4},{6,8},{10,12},{14,16},{18,20},{22,24},{26,28},{30,32},{34,36... | collective-permute-start | bytes 589832 | tf_op jit(solution)/shard_map/ppermute | solution.py:333
  5.7 1.9 %collective-permute-start.1 = (bf16[96,1024]{1,0:T(8,128)(2,1)S(1)}, bf16[96,1024]{1,0:T(8,128)(2,1)S(1)}, u32[]{:S(2)}, u32[]{:S(2)}) collective-permute-start(bf16[96,1024]{1,0:T(8,128)(2,1)S(1)} %get-tuple-element.36), channel_id=1, source_target_pairs={{0,2},{4,6},{8,10},{12,14},{16,18},{20,22},{24,26},{28,30},{32,34}... | collective-permute-start | bytes 589832 | tf_op jit(solution)/shard_map/ppermute | solution.py:338
  7.6 2.3 %shard_map.85 = (bf16[256,1024]{1,0:T(8,128)(2,1)S(1)}, f32[1,1024]{1,0:T(1,128)S(1)}, f32[2,8,128,128]{3,2,1,0:T(8,128)S(1)}, f32[2,8,192,128]{3,2,1,0:T(8,128)...) custom-call(bf16[256,1024]{1,0:T(8,128)(2,1)S(1)} %get-tuple-element.31.k_ref, ...), custom_call_target="tpu_custom_call" | custom-call | flops 1000000000 | bytes 4194304 | tf_op jit(solution)/shard_map/pallas_call | solution.py:316
  9.9 5.3 %collective-permute-done.far_ref = bf16[96,1024]{1,0:T(8,128)(2,1)S(1)} collective-permute-done((bf16[96,1024]{1,0:T(8,128)(2,1)S(1)}, bf16[96,1024]{1,0:T(8,128)(2,1)S(1)}, u32[]{:S(2)}, u32[]{:S(2)}) %collective-permute-start) | collective-permute-done | bytes 196640 | tf_op jit(solution)/shard_map/ppermute | solution.py:333
  15.1 0.0 collective-permute-done.1.near_ref
  15.2 0.9 %shard_map.86 = (bf16[2,96,1024]{2,1,0:T(8,128)(2,1)S(1)}, f32[2,8,64,128]{3,2,1,0:T(8,128)S(1)}, f32[2,8,128]{2,1,0:T(8,128)S(1)}, f32[2,8,128,128]{3,2,1,0:T(8,128)S(1)}, f32[2,256]{1,0:T(2,128)S(1)}) custom-call(bf16[256,1024]{1,0:T(8,128)(2,1)S(1)} %get-tuple-element.34.q_ref, bf16[96,1024]{1,0:T(8,128)(2,1)S(1)} %collective-permute-done.far_ref, ...), custom_call_target="tpu_custom_call" | custom-call | flops 1000000000 | bytes 4194304 | tf_op jit(solution)/shard_map/pallas_call | solution.py:316
  16.0 8.2 %all-gather.1.sums_ref = f32[2,2,256]{2,1,0:T(2,128)S(1)} all-gather(f32[1,2,256]{2,1,0:T(2,128)S(1)} %bitcast.2), channel_id=2, replica_groups=mesh['seq'=256,'head'=2] {'head'}, dimensions={0}, use_global_device_ids=true | all-gather | bytes 6144 | tf_op jit(solution)/shard_map/all_gather | solution.py:379
  24.3 1.4 %shard_map.87 = (bf16[96,1024]{1,0:T(8,128)(2,1)S(1)}, bf16[96,1024]{1,0:T(8,128)(2,1)S(1)}, bf16[2,8,256,128]{3,2,1,0:T(8,128)(2,1)S(1)}, bf16[2,8,128,128]{3,2,1,0:T(8,128)(2,1)S(1)}) custom-call(bf16[256,1024]{1,0:T(8,128)(2,1)S(1)} %get-tuple-element.34.q_ref, bf16[256,1024]{1,0:T(8,128)(2,1)S(1)} %get-tuple-element.32.v_ref, ...), custom_call_target="tpu_custom_call" | custom-call | flops 1000000000 | bytes 4194304 | tf_op jit(solution)/shard_map/pallas_call | solution.py:316
  25.6 3.0 %collective-permute-start.2 = (bf16[96,1024]{1,0:T(8,128)(2,1)S(1)}, bf16[96,1024]{1,0:T(8,128)(2,1)S(1)}, u32[]{:S(2)}, u32[]{:S(2)}) collective-permute-start(bf16[96,1024]{1,0:T(8,128)(2,1)S(1)} %get-tuple-element.54), channel_id=1, source_target_pairs={{2,4},{6,8},{10,12},{14,16},{18,20},{22,24},{26,28},{30,32},{34,36... | collective-permute-start | bytes 589832 | tf_op jit(solution)/shard_map/ppermute | solution.py:333
  28.6 1.9 %collective-permute-start.3 = (bf16[96,1024]{1,0:T(8,128)(2,1)S(1)}, bf16[96,1024]{1,0:T(8,128)(2,1)S(1)}, u32[]{:S(2)}, u32[]{:S(2)}) collective-permute-start(bf16[96,1024]{1,0:T(8,128)(2,1)S(1)} %get-tuple-element.55), channel_id=1, source_target_pairs={{0,2},{4,6},{8,10},{12,14},{16,18},{20,22},{24,26},{28,30},{32,34}... | collective-permute-start | bytes 589832 | tf_op jit(solution)/shard_map/ppermute | solution.py:338
  30.5 2.1 %shard_map.88 = (f32[2,256,1024]{2,1,0:T(8,128)S(1)}, bf16[2,256,48]{2,1,0:T(8,128)(2,1)S(1)}, bf16[256,1024]{1,0:T(8,128)(2,1)}, bf16[256,1024]{1,0:T(8,128)(2,1)}) custom-call(bf16[256,1024]{1,0:T(8,128)(2,1)S(1)} %get-tuple-element.34.q_ref, bf16[256,1024]{1,0:T(8,128)(2,1)S(1)} %get-tuple-element.31.k_ref, ...), custom_call_target="tpu_custom_call" | custom-call | flops 1000000000 | bytes 4194304 | tf_op jit(solution)/shard_map/pallas_call | solution.py:316
  32.6 6.0 %collective-permute-done.2.far_ref = bf16[96,1024]{1,0:T(8,128)(2,1)S(1)} collective-permute-done((bf16[96,1024]{1,0:T(8,128)(2,1)S(1)}, bf16[96,1024]{1,0:T(8,128)(2,1)S(1)}, u32[]{:S(2)}, u32[]{:S(2)}) %collective-permute-start.2) | collective-permute-done | bytes 196640 | tf_op jit(solution)/shard_map/ppermute | solution.py:333
  38.6 0.0 collective-permute-done.3.near_ref
  38.6 1.3 %shard_map.89 = (bf16[256,1024]{1,0:T(8,128)(2,1)}, bf16[256,1024]{1,0:T(8,128)(2,1)}) custom-call(f32[2,256,1024]{2,1,0:T(8,128)S(1)} %get-tuple-element.52.own_ref, bf16[2,256,48]{2,1,0:T(8,128)(2,1)S(1)} %get-tuple-element.53.spread_ref, bf16[96,1024]{1,0:T(8,128)(2,1)S(1)} %collective-permute-done.2.far_ref, ...), custom_call_target="tpu_custom_call" | custom-call | flops 100000000 | bytes 4194304 | tf_op jit(solution)/shard_map/pallas_call | solution.py:316
Async XLA Ops:
  2.1 13.0 %collective-permute-start = (bf16[96,1024]{1,0:T(8,128)(2,1)S(1)}, bf16[96,1024]{1,0:T(8,128)(2,1)S(1)}, u32[]{:S(2)}, u32[]{:S(2)}) collective-permute-start(bf16[96,1024]{1,0:T(8,128)(2,1)S(1)} %get-tuple-element.35), channel_id=1, source_target_pairs={{2,4},{6,8},{10,12},{14,16},{18,20},{22,24},{26,28},{30,32},{34,36... | collective-permute-start | bytes 589832 | tf_op jit(solution)/shard_map/ppermute | solution.py:333
  5.7 9.5 %collective-permute-start.1 = (bf16[96,1024]{1,0:T(8,128)(2,1)S(1)}, bf16[96,1024]{1,0:T(8,128)(2,1)S(1)}, u32[]{:S(2)}, u32[]{:S(2)}) collective-permute-start(bf16[96,1024]{1,0:T(8,128)(2,1)S(1)} %get-tuple-element.36), channel_id=1, source_target_pairs={{0,2},{4,6},{8,10},{12,14},{16,18},{20,22},{24,26},{28,30},{32,34}... | collective-permute-start | bytes 589832 | tf_op jit(solution)/shard_map/ppermute | solution.py:338
  25.6 13.0 %collective-permute-start.2 = (bf16[96,1024]{1,0:T(8,128)(2,1)S(1)}, bf16[96,1024]{1,0:T(8,128)(2,1)S(1)}, u32[]{:S(2)}, u32[]{:S(2)}) collective-permute-start(bf16[96,1024]{1,0:T(8,128)(2,1)S(1)} %get-tuple-element.54), channel_id=1, source_target_pairs={{2,4},{6,8},{10,12},{14,16},{18,20},{22,24},{26,28},{30,32},{34,36... | collective-permute-start | bytes 589832 | tf_op jit(solution)/shard_map/ppermute | solution.py:333
  28.6 10.0 %collective-permute-start.3 = (bf16[96,1024]{1,0:T(8,128)(2,1)S(1)}, bf16[96,1024]{1,0:T(8,128)(2,1)S(1)}, u32[]{:S(2)}, u32[]{:S(2)}) collective-permute-start(bf16[96,1024]{1,0:T(8,128)(2,1)S(1)} %get-tuple-element.55), channel_id=1, source_target_pairs={{0,2},{4,6},{8,10},{12,14},{16,18},{20,22},{24,26},{28,30},{32,34}... | collective-permute-start | bytes 589832 | tf_op jit(solution)/shard_map/ppermute | solution.py:338

commit v4 on v3

v4 whole, which is shorter than its diff:
```python
import jax
import jax.numpy as jnp
from jax import lax
from jax.experimental import pallas as pl
from jax.experimental.pallas import tpu as pltpu
from jax.sharding import PartitionSpec as P

HEADS = 16
HDIM = 128
BLOCK = 16
SCALE = HDIM**-0.5
F32 = jnp.float32
BF16 = jnp.bfloat16

SIDE = 3 * BLOCK
RIM = SIDE + BLOCK
KEPT = BLOCK - 4
PACKED = BLOCK + 2 * KEPT
OWN_RAW = 9 * BLOCK
OWN_MID = 3 * BLOCK
OWN = OWN_RAW + OWN_MID
WINDOW = RIM + OWN
GROUP = 128


def dot(a, b, ca, cb):
    return lax.dot_general(a, b, (((ca,), (cb,)), ((), ())), preferred_element_type=F32)


def parity():
    return lax.axis_index("seq") % 2


def has_sides():
    index = lax.axis_index("seq")
    return (index > 0).astype(jnp.int32), (index < lax.axis_size("seq") - 1).astype(jnp.int32)


def iotas(shape):
    return lax.broadcasted_iota(jnp.int32, shape, 0), lax.broadcasted_iota(jnp.int32, shape, 1)


def one_if(flag, weight=1.0):
    return jnp.where(flag, weight, 0.0)


def pack_entries(p, row, rows, upper):
    middle = (1 - upper) * 4 + upper * (rows // 4 - BLOCK) - BLOCK
    coarse = (1 - upper) * 4 - BLOCK - KEPT
    raw_hit = one_if(p + upper * (rows - BLOCK) == row)
    mid_hit = one_if(p + middle == row // 4, 0.5)
    coarse_hit = one_if(p + coarse == row // 16, 0.25)
    return jnp.where(p < BLOCK, raw_hit, jnp.where(p < BLOCK + KEPT, mid_hit, coarse_hit))


def edge_entries(o, row, rows, upper):
    raw_hit = one_if(o + upper * (rows - BLOCK) == row)
    mid_hit = one_if(o - BLOCK + upper * (rows // 4 - BLOCK) == row // 4, 0.5)
    return jnp.where(o < BLOCK, raw_hit, jnp.where(o < 2 * BLOCK, mid_hit, one_if(o - 2 * BLOCK == row // 16, 0.25)))


def unpack_entries(o, n, upper):
    j, c = o - BLOCK, o - 2 * BLOCK
    from_raw = one_if((n < BLOCK) & (n // 4 == j - 12 * upper), 0.5)
    mid_hit = from_raw + one_if((n >= BLOCK) & (n < BLOCK + KEPT) & (n - BLOCK == j - 4 * (1 - upper)))
    coarse_hit = (
        one_if((n < BLOCK) & (c == 15 * upper), 0.25)
        + one_if((n >= BLOCK) & (n < BLOCK + KEPT) & ((n - BLOCK) // 4 == c - 1 - 11 * upper), 0.5)
        + one_if((n >= BLOCK + KEPT) & (n - BLOCK - KEPT == c - 4 * (1 - upper)))
    )
    return jnp.where(o < BLOCK, one_if(o == n), jnp.where(o < 2 * BLOCK, mid_hit, coarse_hit))


def unpack_both(o, n, upper):
    same = ((o >= SIDE) & (n >= PACKED)) | ((o < SIDE) & (n < PACKED))
    return jnp.where(same, unpack_entries(jnp.where(o >= SIDE, o - SIDE, o), jnp.where(n >= PACKED, n - PACKED, n), upper), 0.0)


def pack_kernel(k_hbm, v_hbm, k_ref, v_ref, far_ref, near_ref, mid_ref, sems):
    copies = [pltpu.make_async_copy(k_hbm, k_ref, sems.at[0]), pltpu.make_async_copy(v_hbm, v_ref, sems.at[1])]
    for copy in copies:
        copy.start()
    rows = k_ref.shape[0]
    mids = rows // 4
    upper = parity()
    out_row, row = iotas((mids, rows))
    parts = [one_if(out_row == row // 4, 0.5)]
    p, row = iotas((PACKED, rows))
    parts += [pack_entries(p, row, rows, edge) for edge in (upper, 1 - upper)]
    pool = jnp.concatenate(parts, axis=0).astype(BF16)
    pooled = []
    for i, ref in enumerate((k_ref, v_ref)):
        copies[i].wait()
        pooled.append(dot(pool, ref[...], 1, 0))
    for at, out_ref in ((mids, far_ref), (mids + PACKED, near_ref)):
        out_ref[...] = jnp.concatenate([x[at : at + PACKED] for x in pooled], axis=0).astype(BF16)
    for i in range(2):
        mid_ref[i] = pooled[i][:mids].astype(BF16)


def own_rows(i, g, cols, raw_ref, mid_ref):
    raw_at, mid_at = (g * (raw_ref.shape[0] - OWN_RAW), g * (mid_ref.shape[1] - OWN_MID))
    return [raw_ref[raw_at : raw_at + OWN_RAW, cols], mid_ref[i, mid_at : mid_at + OWN_MID, cols]]


def side_rows(i, g, cols, side_ref):
    base = i * SIDE
    return [side_ref[g, base : base + SIDE, cols], side_ref[1 - g, base + 2 * BLOCK : base + SIDE, cols]]


def window(i, g, cols, side_ref, raw_ref, mid_ref):
    return jnp.concatenate([*side_rows(i, g, cols, side_ref), *own_rows(i, g, cols, raw_ref, mid_ref)], axis=0)


def allowed(g, has_below, has_above):
    shape = (WINDOW, GROUP)
    kb = lax.broadcasted_iota(jnp.int32, shape, 0) // BLOCK
    qb = lax.broadcasted_iota(jnp.int32, shape, 1) // BLOCK
    qm = qb // 4
    raw_gap = kb - 4 - g - qb
    mid_gap = kb - 13 - g - qm
    edge_raw = qb == (7 if g else 0)
    edge_mid = qm == (1 if g else 0)
    one = jnp.ones(shape, jnp.int32)
    none = jnp.zeros(shape, jnp.int32)
    own = jnp.where(kb < 13, jnp.where(jnp.abs(raw_gap) <= 1, one, none), jnp.where(jnp.abs(mid_gap) == 1, one, none))
    side = jnp.where(kb == 0, jnp.where(edge_raw, one, none), jnp.where(kb == 1, jnp.where(edge_mid, one, none), one))
    valid_side, valid_other = (has_above, has_below) if g else (has_below, has_above)
    return jnp.where(kb < 3, side * valid_side, jnp.where(kb == 3, one * valid_other, own))


def local_kernel(
    k_ref, v_ref, mid_ref, q_hbm, cot_hbm, gain_hbm,
    q_ref, gain_ref, scaled_ref, lifted_ref, stats_ref, mix_ref, bias_ref, unfold_ref, fold_ref, cot_ref, own_bias, sems,
):
    copies = [
        pltpu.make_async_copy(src, dst, sems.at[n])
        for n, (src, dst) in enumerate([(q_hbm, q_ref), (cot_hbm, cot_ref), (gain_hbm, gain_ref)])
    ]
    for copy in copies:
        copy.start()
    for g in range(2):
        bias = jnp.where(allowed(g, *has_sides()) == 1, 0.0, -1e30)
        bias_ref[g] = bias[:RIM]
        own_bias[g] = bias[RIM:]
        unfold_ref[g] = unpack_both(*iotas((2 * SIDE, 2 * PACKED)), 1 - g).astype(BF16)
        fold_ref[g] = unpack_both(*iotas((2 * PACKED, 2 * SIDE))[::-1], 1 - g).astype(BF16)
    for copy in copies:
        copy.wait()
    heads = lifted_ref.shape[1]
    for g in range(2):
        rows = slice(g * GROUP, (g + 1) * GROUP)
        for h in range(heads):
            cols = slice(h * HDIM, (h + 1) * HDIM)
            keys = jnp.concatenate(own_rows(0, g, cols, k_ref, mid_ref), axis=0)
            scores = dot(keys, q_ref[rows, cols], 1, 1) * SCALE + own_bias[g]
            highest = jnp.max(scores, axis=0, keepdims=True)
            lifted = jnp.exp(scores - highest).astype(BF16)
            lifted_ref[g, h] = lifted
            stats_ref[g, h : h + 1] = highest
            stats_ref[g, heads + h : heads + h + 1] = jnp.sum(lifted.astype(F32), axis=0, keepdims=True)
            scaled_ref[g, h] = (cot_ref[rows, cols].astype(F32) * gain_ref[:, cols]).T
    for g in range(2):
        for h in range(heads):
            values = jnp.concatenate(own_rows(1, g, slice(h * HDIM, (h + 1) * HDIM), v_ref, mid_ref), axis=0)
            mix_ref[g, h] = dot(values, lifted_ref[g, h], 0, 0)


def forward_kernel(
    q_ref, far_ref, near_ref, bias_ref, unfold_ref, scaled_ref, stats_ref, mix_ref,
    side_ref, side_lifted, own_scale, side_scale, att_ref, sums_ref, side_stats,
):
    odd = parity()
    side_ref[odd] = dot(unfold_ref[odd], far_ref[...], 1, 0).astype(BF16)
    side_ref[1 - odd] = dot(unfold_ref[1 - odd], near_ref[...], 1, 0).astype(BF16)
    heads = mix_ref.shape[1]
    for g in range(2):
        rows = slice(g * GROUP, (g + 1) * GROUP)
        for h in range(heads):
            cols = slice(h * HDIM, (h + 1) * HDIM)
            keys = jnp.concatenate(side_rows(0, g, cols, side_ref), axis=0)
            scores = dot(keys, q_ref[rows, cols], 1, 1) * SCALE + bias_ref[g]
            highest = jnp.max(scores, axis=0, keepdims=True)
            lifted = jnp.exp(scores - highest).astype(BF16)
            side_lifted[g, h] = lifted
            side_stats[g, h : h + 1] = highest
            side_stats[g, heads + h : heads + h + 1] = jnp.sum(lifted.astype(F32), axis=0, keepdims=True)
    for g in range(2):
        rows = slice(g * GROUP, (g + 1) * GROUP)
        own_high, side_high = stats_ref[g, :heads], side_stats[g, :heads]
        highest = jnp.maximum(own_high, side_high)
        own_part, side_part = jnp.exp(own_high - highest), jnp.exp(side_high - highest)
        inverse = 1.0 / (stats_ref[g, heads:] * own_part + side_stats[g, heads:] * side_part)
        own_part, side_part = own_part * inverse, side_part * inverse
        own_scale[g] = own_part
        side_scale[g] = side_part
        squares = jnp.zeros((HDIM, GROUP), F32)
        crossed = jnp.zeros((HDIM, GROUP), F32)
        for h in range(heads):
            cols = slice(h * HDIM, (h + 1) * HDIM)
            values = jnp.concatenate(side_rows(1, g, cols, side_ref), axis=0)
            mixed = mix_ref[g, h] * own_part[h : h + 1] + dot(values, side_lifted[g, h], 0, 0) * side_part[h : h + 1]
            att_ref[g, h] = mixed
            squares += mixed * mixed
            crossed += mixed * scaled_ref[g, h]
        sums_ref[0:1, rows] = jnp.sum(squares, axis=0, keepdims=True)
        sums_ref[1:2, rows] = jnp.sum(crossed, axis=0, keepdims=True)


def row_factors(sums_ref):
    feat_all = HEADS * HDIM
    totals = sums_ref[0] + sums_ref[1]
    factor = lax.rsqrt(totals[0:1] / feat_all + 1e-06)
    return factor, factor * factor * factor * totals[1:2] / feat_all


def side_piece(g, q_ref, side_w, ds_ref, dout_ref, out_ref):
    half = q_ref.shape[0] // 2
    mine = pl.ds(pl.multiple_of(g * half, half), half)
    other = pl.ds(pl.multiple_of((1 - g) * half, half), half)
    blank = jnp.zeros((2 * BLOCK, GROUP), BF16)
    for h in range(side_w.shape[1]):
        cols = slice(h * HDIM, (h + 1) * HDIM)
        lefts = [
            jnp.concatenate([ref[g, h, :SIDE], jnp.concatenate([blank, ref[1 - g, h, SIDE:RIM]], axis=0)], axis=1)
            for ref in (ds_ref, side_w)
        ]
        queries = jnp.concatenate([q_ref[mine, cols], q_ref[other, cols]], axis=0)
        out_ref[:SIDE, cols] = dot(lefts[0], queries, 1, 0).astype(BF16)
        douts = jnp.concatenate([dout_ref[g, h], dout_ref[1 - g, h]], axis=1)
        out_ref[SIDE:, cols] = dot(lefts[1], douts, 1, 1).astype(BF16)


def pieces_kernel(
    q_ref, side_ref, scaled_ref, side_lifted, side_scale, att_ref, sums_ref,
    far_out, ds_ref, side_w, dout_ref, delta_ref,
):
    factor, cross = row_factors(sums_ref)
    heads = side_w.shape[1]
    for h in range(heads):
        cols = slice(h * HDIM, (h + 1) * HDIM)
        for g in range(2):
            rows = slice(g * GROUP, (g + 1) * GROUP)
            attended = att_ref[g, h]
            grad_out = (factor[:, rows] * scaled_ref[g, h] - cross[:, rows] * attended).astype(BF16)
            dout_ref[g, h] = grad_out
            delta = jnp.sum(grad_out.astype(F32) * attended, axis=0, keepdims=True)
            delta_ref[g, h : h + 1] = delta
            values = jnp.concatenate(side_rows(1, g, cols, side_ref), axis=0)
            weights = side_lifted[g, h].astype(F32) * side_scale[g, h : h + 1]
            side_w[g, h] = weights.astype(BF16)
            ds_ref[g, h] = (weights * (dot(values, grad_out, 1, 0) - delta) * SCALE).astype(BF16)
    side_piece(parity(), q_ref, side_w, ds_ref, dout_ref, far_out)


def near_kernel(q_ref, side_w, ds_ref, dout_ref, fold_ref, near_out, piece_ref):
    side = 1 - parity()
    side_piece(side, q_ref, side_w, ds_ref, dout_ref, piece_ref)
    near_out[...] = dot(fold_ref[side], piece_ref[...], 1, 0).astype(BF16)


def own_kernel(
    q_ref, k_ref, v_ref, mid_ref, side_ref, gain_ref, lifted_ref, own_scale, att_ref, sums_ref, ds_ref, dout_ref, delta_ref,
    own_ref, mid_grad, spread_ref, normed_hbm, dq_hbm, normed_ref, dq_ref, own_w, own_ds, sems,
):
    odd = parity()
    rows_all = q_ref.shape[0]
    heads = lifted_ref.shape[1]
    for h in range(heads):
        cols = slice(h * HDIM, (h + 1) * HDIM)
        for g in range(2):
            values = jnp.concatenate(own_rows(1, g, cols, v_ref, mid_ref), axis=0)
            weights = lifted_ref[g, h].astype(F32) * own_scale[g, h : h + 1]
            own_w[g, h] = weights.astype(BF16)
            own_ds[g, h] = (weights * (dot(values, dout_ref[g, h], 1, 0) - delta_ref[g, h : h + 1]) * SCALE).astype(BF16)
    factor, _ = row_factors(sums_ref)
    copies = []
    half = heads // 2
    for h in range(heads):
        cols = slice(h * HDIM, (h + 1) * HDIM)
        for g in range(2):
            rows = slice(g * GROUP, (g + 1) * GROUP)
            normed_ref[rows, cols] = ((att_ref[g, h] * factor[:, rows]).T * gain_ref[:, cols]).astype(BF16)
            keys = window(0, g, cols, side_ref, k_ref, mid_ref)
            dq_ref[rows, cols] = dot(jnp.concatenate([ds_ref[g, h], own_ds[g, h]], axis=0), keys, 0, 0).astype(BF16)
        if h % half == half - 1:
            done = pl.ds((h + 1 - half) * HDIM, half * HDIM)
            for ref, hbm in ((normed_ref, normed_hbm), (dq_ref, dq_hbm)):
                copies.append(pltpu.make_async_copy(ref.at[:, done], hbm.at[:, done], sems.at[len(copies)]))
                copies[-1].start()
    both_raw = 2 * OWN_RAW - rows_all
    both_mid = 2 * OWN_MID - rows_all // 4
    for h in range(heads):
        cols = slice(h * HDIM, (h + 1) * HDIM)
        inner = []
        for g in range(2):
            rows = slice(g * GROUP, (g + 1) * GROUP)
            inner.append((dot(own_ds[g, h], q_ref[rows, cols], 1, 0), dot(own_w[g, h], dout_ref[g, h], 1, 1)))
        for i in range(2):
            lower, upper = inner[0][i], inner[1][i]
            own_ref[i, :, cols] = jnp.concatenate(
                [lower[: OWN_RAW - both_raw], lower[OWN_RAW - both_raw : OWN_RAW] + upper[:both_raw], upper[both_raw:OWN_RAW]],
                axis=0,
            )
            low_mid, up_mid = lower[OWN_RAW:], upper[OWN_RAW:]
            mid_grad[i, :, cols] = jnp.concatenate(
                [low_mid[: OWN_MID - both_mid], low_mid[OWN_MID - both_mid :] + up_mid[:both_mid], up_mid[both_mid:]], axis=0
            ).astype(BF16)
    row, p = iotas((rows_all, PACKED))
    near_part = pack_entries(p, row, rows_all, 1 - odd)
    row, o = iotas((rows_all, SIDE))
    far_part = edge_entries(o, row, rows_all, odd)
    no_near, no_far = jnp.zeros((rows_all, PACKED), F32), jnp.zeros((rows_all, SIDE), F32)
    row, at = iotas((rows_all, rows_all // 4))
    mid_part = one_if(row // 4 == at, 0.5)
    spread_ref[0] = jnp.concatenate([far_part, no_far, near_part, no_near, mid_part], axis=1).astype(BF16)
    spread_ref[1] = jnp.concatenate([no_far, far_part, no_near, near_part, mid_part], axis=1).astype(BF16)
    for copy in copies:
        copy.wait()


def final_kernel(own_ref, mid_grad, spread_ref, far_ref, near_ref, dk_hbm, dv_hbm, dk_ref, dv_ref, sems):
    rows = own_ref.shape[1]
    copies = []
    for i, (out_ref, hbm) in enumerate(((dk_ref, dk_hbm), (dv_ref, dv_hbm))):
        got = jnp.concatenate([far_ref[...], near_ref[...], mid_grad[i]], axis=0)
        for part in range(2):
            at = slice(part * (rows // 2), (part + 1) * (rows // 2))
            out_ref[at] = (own_ref[i, at] + dot(spread_ref[i, at], got, 1, 0)).astype(BF16)
            copies.append(pltpu.make_async_copy(out_ref.at[at], hbm.at[at], sems.at[len(copies)]))
            copies[-1].start()
    for copy in copies:
        copy.wait()


VMEM = pl.BlockSpec(memory_space=pltpu.VMEM)
HBM = pl.BlockSpec(memory_space=pltpu.HBM)


def call(kernel, args, outs, scratch, flops):
    placed = [pltpu.with_memory_space_constraint(x, pltpu.HBM) if space is HBM else x for x, space in args]
    return pl.pallas_call(
        kernel,
        out_shape=tuple(shape for shape, _ in outs),
        in_specs=[space for _, space in args],
        out_specs=tuple(space for _, space in outs),
        scratch_shapes=scratch,
        compiler_params=pltpu.CompilerParams(vmem_limit_bytes=24 * 2**20),
        cost_estimate=pl.CostEstimate(flops=flops, bytes_accessed=flops // 256, transcendentals=0),
    )(*placed)


def on(space, *xs):
    return [(x, space) for x in xs]


def far_swap(x):
    pairs = [(i, i + 1) for i in range(1, lax.axis_size("seq") - 1, 2)]
    return lax.ppermute(x, "seq", pairs + [(j, i) for i, j in pairs])


def near_swap(x):
    pairs = [(i, i + 1) for i in range(0, lax.axis_size("seq"), 2)]
    return lax.ppermute(x, "seq", pairs + [(j, i) for i, j in pairs])


def local(queries, key_vectors, value_vectors, norm_gain, cotangent):
    rows, feats = queries.shape
    heads = feats // HDIM
    gain = norm_gain.reshape(1, feats)
    arr = jax.ShapeDtypeStruct
    dma = pltpu.SemaphoreType.DMA
    whole = arr((rows, feats), BF16)
    packed = arr((2 * PACKED, feats), BF16)
    mids = arr((2, rows // 4, feats), BF16)
    sides = pltpu.VMEM((2 * SIDE, feats), BF16)
    tiles = arr((2, heads, HDIM, GROUP), F32)
    k, v, far, near, mid = call(
        pack_kernel,
        on(HBM, key_vectors, value_vectors),
        on(VMEM, whole, whole, packed, packed, mids),
        [dma((2,))],
        10**8,
    )
    far_got = far_swap(far)
    near_got = near_swap(near)
    q, gain, scaled, lifted, stats, mix, bias, unfold, fold = call(
        local_kernel,
        on(VMEM, k, v, mid) + on(HBM, queries, cotangent, gain),
        on(
            VMEM, whole, arr((1, feats), F32), tiles, arr((2, heads, OWN, GROUP), BF16), arr((2, 2 * heads, GROUP), F32),
            tiles, arr((2, RIM, GROUP), F32), arr((2, 2 * SIDE, 2 * PACKED), BF16), arr((2, 2 * PACKED, 2 * SIDE), BF16),
        ),
        [pltpu.VMEM((rows, feats), BF16), pltpu.VMEM((2, OWN, GROUP), F32), dma((3,))],
        10**9,
    )
    scales = arr((2, heads, GROUP), F32)
    side_tiles = arr((2, heads, RIM, GROUP), BF16)
    rim = arr((2 * SIDE, feats), BF16)
    side, side_lifted, own_scale, side_scale, attended, sums = call(
        forward_kernel,
        on(VMEM, q, far_got, near_got, bias, unfold, scaled, stats, mix),
        on(VMEM, arr((2, 2 * SIDE, feats), BF16), side_tiles, scales, scales, tiles, arr((2, rows), F32)),
        [pltpu.VMEM((2, 2 * heads, GROUP), F32)],
        10**9,
    )
    sums = lax.all_gather(sums, "head")
    far_piece, ds, side_w, dout, delta = call(
        pieces_kernel,
        on(VMEM, q, side, scaled, side_lifted, side_scale, attended, sums),
        on(VMEM, rim, side_tiles, side_tiles, arr((2, heads, HDIM, GROUP), BF16), scales),
        [],
        10**9,
    )
    far_back = far_swap(far_piece)
    (near_piece,) = call(near_kernel, on(VMEM, q, side_w, ds, dout, fold), on(VMEM, packed), [sides], 10**9)
    near_back = near_swap(near_piece)
    own_tiles = pltpu.VMEM((2, heads, OWN, GROUP), BF16)
    own, mid_grad, spread, normed, query_grad = call(
        own_kernel,
        on(VMEM, q, k, v, mid, side, gain, lifted, own_scale, attended, sums, ds, dout, delta),
        on(VMEM, arr((2, rows, feats), F32), mids, arr((2, rows, 2 * SIDE + 2 * PACKED + rows // 4), BF16)) + on(HBM, whole, whole),
        [pltpu.VMEM((rows, feats), BF16), pltpu.VMEM((rows, feats), BF16), own_tiles, own_tiles, dma((4,))],
        10**6,
    )
    key_grad, value_grad = call(
        final_kernel,
        on(VMEM, own, mid_grad, spread, far_back, near_back),
        on(HBM, whole, whole),
        [pltpu.VMEM((rows, feats), BF16), pltpu.VMEM((rows, feats), BF16), dma((4,))],
        10**8,
    )
    return normed, query_grad, key_grad, value_grad


def solution(mesh):
    in_specs = (P("seq", "head"), P("seq", "head"), P("seq", "head"), P("head"), P("seq", "head"))
    out_specs = (P("seq", "head"), P("seq", "head"), P("seq", "head"), P("seq", "head"))
    return jax.shard_map(local, mesh=mesh, in_specs=in_specs, out_specs=out_specs, check_vma=False)
```

time: 40.1 us -> 39.3 us (0.980)
  the two profiles are of different devices: /device:TPU:288 before, /device:TPU:256 now
where the time goes in v4:
time: 39.3 us; the launch traced here: 39.1 us
  starting transfers between devices  15.2 us (39%)
  Pallas kernels  9.77 us (25%)
  blocking collectives  8.25 us (21%)
  waiting for transfers between devices  5.23 us (13%)
  between operations  0.71 us (2%)
    ppermute x2, starting transfers between devices, far_swap(): return lax.ppermute(x, 'seq', pairs + [(j, i) for i, j in pairs])  11.3 us
    pallas_call x7, Pallas kernels, call(): pl.pallas_call(kernel, out_shape=tuple((shape for shape, _ in outs)), in_...  9.77 us
    all_gather x1, blocking collectives, local(): sums = lax.all_gather(sums, 'head')  8.25 us
    ppermute x2, waiting for transfers between devices, far_swap(): return lax.ppermute(x, 'seq', pairs + [(j, i) for i, j in pairs])  5.22 us
    ppermute x2, starting transfers between devices, near_swap(): return lax.ppermute(x, 'seq', pairs + [(j, i) for i, j in pairs])  3.84 us
  transfers between devices with their start and end apart: 4, of which 2 were waited for; matrix products, arithmetic and copies ran while one was open for 0% of the time, Pallas kernels for 13%

profile of v4, /device:TPU:256, one launch (start us, length us, event | category | flops | bytes accessed | tf_op | source)
XLA Modules:
  0.0 39.1 jit_solution(9285500279608432004)
XLA Ops:
  0.6 1.6 %shard_map.84 = (bf16[256,1024]{1,0:T(8,128)(2,1)S(1)}, bf16[256,1024]{1,0:T(8,128)(2,1)S(1)}, bf16[80,1024]{1,0:T(8,128)(2,1)S(1)}, bf16[80,1024]{1,0:T(8,128)(2,1)S(1)}, bf16[2,64,1024]{2,1,0:T(8,128)(2,1)S(1)}) custom-call(bf16[256,1024]{1,0:T(8,128)(2,1)} %k_hbm.1, bf16[256,1024]{1,0:T(8,128)(2,1)} %v_hbm.1), custom_call_target="tpu_custom_call" | custom-call | flops 100000000 | bytes 390625 | tf_op jit(solution)/shard_map/pallas_call | solution.py:342
  2.2 6.2 %collective-permute-start = (bf16[80,1024]{1,0:T(8,128)(2,1)S(1)}, bf16[80,1024]{1,0:T(8,128)(2,1)S(1)}, u32[]{:S(2)}, u32[]{:S(2)}) collective-permute-start(bf16[80,1024]{1,0:T(8,128)(2,1)S(1)} %get-tuple-element.40), channel_id=1, source_target_pairs={{2,4},{6,8},{10,12},{14,16},{18,20},{22,24},{26,28},{30,32},{34,36... | collective-permute-start | bytes 491528 | tf_op jit(solution)/shard_map/ppermute | solution.py:359
  8.5 1.9 %collective-permute-start.1 = (bf16[80,1024]{1,0:T(8,128)(2,1)S(1)}, bf16[80,1024]{1,0:T(8,128)(2,1)S(1)}, u32[]{:S(2)}, u32[]{:S(2)}) collective-permute-start(bf16[80,1024]{1,0:T(8,128)(2,1)S(1)} %get-tuple-element.41), channel_id=1, source_target_pairs={{0,2},{4,6},{8,10},{12,14},{16,18},{20,22},{24,26},{28,30},{32,34}... | collective-permute-start | bytes 491528 | tf_op jit(solution)/shard_map/ppermute | solution.py:364
  10.4 2.4 %shard_map.85 = (bf16[256,1024]{1,0:T(8,128)(2,1)S(1)}, f32[1,1024]{1,0:T(1,128)S(1)}, f32[2,8,128,128]{3,2,1,0:T(8,128)S(1)}, bf16[2,8,192,128]{3,2,1,0:T(8,128...) custom-call(bf16[256,1024]{1,0:T(8,128)(2,1)S(1)} %get-tuple-element, ...), custom_call_target="tpu_custom_call" | custom-call | flops 1000000000 | bytes 3906250 | tf_op jit(solution)/shard_map/pallas_call | solution.py:342
  12.8 2.1 %collective-permute-done.far_ref = bf16[80,1024]{1,0:T(8,128)(2,1)S(1)} collective-permute-done((bf16[80,1024]{1,0:T(8,128)(2,1)S(1)}, bf16[80,1024]{1,0:T(8,128)(2,1)S(1)}, u32[]{:S(2)}, u32[]{:S(2)}) %collective-permute-start) | collective-permute-done | bytes 163872 | tf_op jit(solution)/shard_map/ppermute | solution.py:359
  14.9 0.0 collective-permute-done.1.near_ref
  14.9 1.1 %shard_map.86 = (bf16[2,96,1024]{2,1,0:T(8,128)(2,1)S(1)}, bf16[2,8,64,128]{3,2,1,0:T(8,128)(2,1)S(1)}, f32[2,8,128]{2,1,0:T(8,128)S(1)}, f32[2,8,128]{2,1,0:T(8...) custom-call(bf16[256,1024]{1,0:T(8,128)(2,1)S(1)} %get-tuple-element.39.q_ref, ...), custom_call_target="tpu_custom_call" | custom-call | flops 1000000000 | bytes 3906250 | tf_op jit(solution)/shard_map/pallas_call | solution.py:342
  15.9 8.2 %all-gather.1.sums_ref = f32[2,2,256]{2,1,0:T(2,128)S(1)} all-gather(f32[1,2,256]{2,1,0:T(2,128)S(1)} %bitcast.2), channel_id=2, replica_groups=mesh['seq'=256,'head'=2] {'head'}, dimensions={0}, use_global_device_ids=true | all-gather | bytes 6144 | tf_op jit(solution)/shard_map/all_gather | solution.py:407
  24.2 0.7 %shard_map.87 = (bf16[96,1024]{1,0:T(8,128)(2,1)S(1)}, bf16[2,8,64,128]{3,2,1,0:T(8,128)(2,1)S(1)}, bf16[2,8,64,128]{3,2,1,0:T(8,128)(2,1)S(1)}, bf16[2,8,128,128]{3,2,1,0:T(8,128)(2,1)S(1)}, f32[2,8,128]{2,1,0:T(8,128)S(1)}) custom-call(bf16[256,1024]{1,0:T(8,128)(2,1)S(1)} %get-tuple-element.39.q_ref, bf16[2,96,1024]{2,1,0:T(8,128)(2,1)S(1)} %get-tuple-element.47.side_ref, ...), custom_call_target="tpu_custom_call" | custom-call | flops 1000000000 | bytes 3906250 | tf_op jit(solution)/shard_map/pallas_call | solution.py:342
  24.9 5.1 %collective-permute-start.2 = (bf16[96,1024]{1,0:T(8,128)(2,1)S(1)}, bf16[96,1024]{1,0:T(8,128)(2,1)S(1)}, u32[]{:S(2)}, u32[]{:S(2)}) collective-permute-start(bf16[96,1024]{1,0:T(8,128)(2,1)S(1)} %get-tuple-element.63), channel_id=1, source_target_pairs={{2,4},{6,8},{10,12},{14,16},{18,20},{22,24},{26,28},{30,32},{34,36... | collective-permute-start | bytes 589832 | tf_op jit(solution)/shard_map/ppermute | solution.py:359
  30.0 0.6 %shard_map.89 = bf16[80,1024]{1,0:T(8,128)(2,1)S(1)} custom-call(bf16[256,1024]{1,0:T(8,128)(2,1)S(1)} %get-tuple-element.39.q_ref, bf16[2,8,64,128]{3,2,1,0:T(8,128)(2,1)S(1)} %get-tuple-element.64.side_w, bf16[2,8,64,128]{3,2,1,0:T(8,128)(2,1)S(1)} %get-tuple-element.55.ds_ref, bf16[2,8,128,128]{3,2,1,0:T(8,128)(2,1)S(1)} %get-tuple-element.56.dout_ref, ...), custom_call_target="tpu_custom_call" | custom-call | flops 1000000000 | bytes 3906250 | tf_op jit(solution)/shard_map/pallas_call | solution.py:342
  30.5 1.9 %collective-permute-start.3 = (bf16[80,1024]{1,0:T(8,128)(2,1)S(1)}, bf16[80,1024]{1,0:T(8,128)(2,1)S(1)}, u32[]{:S(2)}, u32[]{:S(2)}) collective-permute-start(bf16[80,1024]{1,0:T(8,128)(2,1)S(1)} %shard_map.89), channel_id=1, source_target_pairs={{0,2},{4,6},{8,10},{12,14},{16,18},{20,22},{24,26},{28,30},{32,34}... | collective-permute-start | bytes 491528 | tf_op jit(solution)/shard_map/ppermute | solution.py:364
  32.5 2.3 %shard_map.88 = (f32[2,256,1024]{2,1,0:T(8,128)S(1)}, bf16[2,64,1024]{2,1,0:T(8,128)(2,1)S(1)}, bf16[2,256,240]{2,1,0:T(8,128)(2,1)S(1)}, bf16[256,1024]{1,0:T(8,128)(2,1)}, bf16[256,1024]{1,0:T(8,128)(2,1)}) custom-call(bf16[256,1024]{1,0:T(8,128)(2,1)S(1)} %get-tuple-element.39.q_ref, bf16[256,1024]{1,0:T(8,128)(2,1)S(1)} %get-tuple-element.36.k_ref, ...), custom_call_target="tpu_custom_call" | custom-call | flops 1000000 | bytes 3906 | tf_op jit(solution)/shard_map/pallas_call | solution.py:342
  34.7 0.0 collective-permute-done.3.near_ref
  34.8 3.1 %collective-permute-done.2.far_ref = bf16[96,1024]{1,0:T(8,128)(2,1)S(1)} collective-permute-done((bf16[96,1024]{1,0:T(8,128)(2,1)S(1)}, bf16[96,1024]{1,0:T(8,128)(2,1)S(1)}, u32[]{:S(2)}, u32[]{:S(2)}) %collective-permute-start.2) | collective-permute-done | bytes 196640 | tf_op jit(solution)/shard_map/ppermute | solution.py:359
  37.9 1.2 %shard_map.90 = (bf16[256,1024]{1,0:T(8,128)(2,1)}, bf16[256,1024]{1,0:T(8,128)(2,1)}) custom-call(f32[2,256,1024]{2,1,0:T(8,128)S(1)} %get-tuple-element.60.own_ref, bf16[2,64,1024]{2,1,0:T(8,128)(2,1)S(1)} %get-tuple-element.61.mid_grad, bf16[2,256,240]{2,1,0:T(8,128)(2,1)S(1)} %get-tuple-element.62.spread_ref, ...), custom_call_target="tpu_custom_call" | custom-call | flops 100000000 | bytes 390625 | tf_op jit(solution)/shard_map/pallas_call | solution.py:342
Async XLA Ops:
  2.2 12.7 %collective-permute-start = (bf16[80,1024]{1,0:T(8,128)(2,1)S(1)}, bf16[80,1024]{1,0:T(8,128)(2,1)S(1)}, u32[]{:S(2)}, u32[]{:S(2)}) collective-permute-start(bf16[80,1024]{1,0:T(8,128)(2,1)S(1)} %get-tuple-element.40), channel_id=1, source_target_pairs={{2,4},{6,8},{10,12},{14,16},{18,20},{22,24},{26,28},{30,32},{34,36... | collective-permute-start | bytes 491528 | tf_op jit(solution)/shard_map/ppermute | solution.py:359
  8.5 6.4 %collective-permute-start.1 = (bf16[80,1024]{1,0:T(8,128)(2,1)S(1)}, bf16[80,1024]{1,0:T(8,128)(2,1)S(1)}, u32[]{:S(2)}, u32[]{:S(2)}) collective-permute-start(bf16[80,1024]{1,0:T(8,128)(2,1)S(1)} %get-tuple-element.41), channel_id=1, source_target_pairs={{0,2},{4,6},{8,10},{12,14},{16,18},{20,22},{24,26},{28,30},{32,34}... | collective-permute-start | bytes 491528 | tf_op jit(solution)/shard_map/ppermute | solution.py:364
  24.9 13.0 %collective-permute-start.2 = (bf16[96,1024]{1,0:T(8,128)(2,1)S(1)}, bf16[96,1024]{1,0:T(8,128)(2,1)S(1)}, u32[]{:S(2)}, u32[]{:S(2)}) collective-permute-start(bf16[96,1024]{1,0:T(8,128)(2,1)S(1)} %get-tuple-element.63), channel_id=1, source_target_pairs={{2,4},{6,8},{10,12},{14,16},{18,20},{22,24},{26,28},{30,32},{34,36... | collective-permute-start | bytes 589832 | tf_op jit(solution)/shard_map/ppermute | solution.py:359
  30.5 4.2 %collective-permute-start.3 = (bf16[80,1024]{1,0:T(8,128)(2,1)S(1)}, bf16[80,1024]{1,0:T(8,128)(2,1)S(1)}, u32[]{:S(2)}, u32[]{:S(2)}) collective-permute-start(bf16[80,1024]{1,0:T(8,128)(2,1)S(1)} %shard_map.89), channel_id=1, source_target_pairs={{0,2},{4,6},{8,10},{12,14},{16,18},{20,22},{24,26},{28,30},{32,34}... | collective-permute-start | bytes 491528 | tf_op jit(solution)/shard_map/ppermute | solution.py:364

commit v5 on v4

--- a/solution.py
+++ b/solution.py
@@ -16,6 +16,7 @@
 RIM = SIDE + BLOCK
 KEPT = BLOCK - 4
 PACKED = BLOCK + 2 * KEPT
+PARTS = 2
 OWN_RAW = 9 * BLOCK
 OWN_MID = 3 * BLOCK
 OWN = OWN_RAW + OWN_MID
@@ -131,7 +132,7 @@
 
 def local_kernel(
     k_ref, v_ref, mid_ref, q_hbm, cot_hbm, gain_hbm,
-    q_ref, gain_ref, scaled_ref, lifted_ref, stats_ref, mix_ref, bias_ref, unfold_ref, fold_ref, cot_ref, own_bias, sems,
+    q_ref, gain_ref, scaled_ref, lifted_ref, stats_ref, mix_ref, bias_ref, unfold_ref, fold_ref, spread_ref, cot_ref, own_bias, sems,
 ):
     copies = [
         pltpu.make_async_copy(src, dst, sems.at[n])
@@ -145,6 +146,17 @@
         own_bias[g] = bias[RIM:]
         unfold_ref[g] = unpack_both(*iotas((2 * SIDE, 2 * PACKED)), 1 - g).astype(BF16)
         fold_ref[g] = unpack_both(*iotas((2 * PACKED, 2 * SIDE))[::-1], 1 - g).astype(BF16)
+    odd = parity()
+    rows_all = q_ref.shape[0]
+    row, p = iotas((rows_all, PACKED))
+    near_part = pack_entries(p, row, rows_all, 1 - odd)
+    row, o = iotas((rows_all, SIDE))
+    far_part = edge_entries(o, row, rows_all, odd)
+    no_near, no_far = jnp.zeros((rows_all, PACKED), F32), jnp.zeros((rows_all, SIDE), F32)
+    row, at = iotas((rows_all, rows_all // 4))
+    mid_part = one_if(row // 4 == at, 0.5)
+    spread_ref[0] = jnp.concatenate([far_part, no_far, near_part, no_near, mid_part], axis=1).astype(BF16)
+    spread_ref[1] = jnp.concatenate([no_far, far_part, no_near, near_part, mid_part], axis=1).astype(BF16)
     for copy in copies:
         copy.wait()
     heads = lifted_ref.shape[1]
@@ -261,9 +273,8 @@
 
 def own_kernel(
     q_ref, k_ref, v_ref, mid_ref, side_ref, gain_ref, lifted_ref, own_scale, att_ref, sums_ref, ds_ref, dout_ref, delta_ref,
-    own_ref, mid_grad, spread_ref, normed_hbm, dq_hbm, normed_ref, dq_ref, own_w, own_ds, sems,
+    own_ref, mid_grad, normed_hbm, dq_hbm, normed_ref, dq_ref, own_w, own_ds, sems,
 ):
-    odd = parity()
     rows_all = q_ref.shape[0]
     heads = lifted_ref.shape[1]
     for h in range(heads):
@@ -306,28 +317,19 @@
             mid_grad[i, :, cols] = jnp.concatenate(
                 [low_mid[: OWN_MID - both_mid], low_mid[OWN_MID - both_mid :] + up_mid[:both_mid], up_mid[both_mid:]], axis=0
             ).astype(BF16)
-    row, p = iotas((rows_all, PACKED))
-    near_part = pack_entries(p, row, rows_all, 1 - odd)
-    row, o = iotas((rows_all, SIDE))
-    far_part = edge_entries(o, row, rows_all, odd)
-    no_near, no_far = jnp.zeros((rows_all, PACKED), F32), jnp.zeros((rows_all, SIDE), F32)
-    row, at = iotas((rows_all, rows_all // 4))
-    mid_part = one_if(row // 4 == at, 0.5)
-    spread_ref[0] = jnp.concatenate([far_part, no_far, near_part, no_near, mid_part], axis=1).astype(BF16)
-    spread_ref[1] = jnp.concatenate([no_far, far_part, no_near, near_part, mid_part], axis=1).astype(BF16)
     for copy in copies:
         copy.wait()
 
 
 def final_kernel(own_ref, mid_grad, spread_ref, far_ref, near_ref, dk_hbm, dv_hbm, dk_ref, dv_ref, sems):
-    rows = own_ref.shape[1]
+    width = own_ref.shape[2] // PARTS
     copies = []
     for i, (out_ref, hbm) in enumerate(((dk_ref, dk_hbm), (dv_ref, dv_hbm))):
-        got = jnp.concatenate([far_ref[...], near_ref[...], mid_grad[i]], axis=0)
-        for part in range(2):
-            at = slice(part * (rows // 2), (part + 1) * (rows // 2))
-            out_ref[at] = (own_ref[i, at] + dot(spread_ref[i, at], got, 1, 0)).astype(BF16)
-            copies.append(pltpu.make_async_copy(out_ref.at[at], hbm.at[at], sems.at[len(copies)]))
+        for part in range(PARTS):
+            at = slice(part * width, (part + 1) * width)
+            got = jnp.concatenate([far_ref[:, at], near_ref[:, at], mid_grad[i, :, at]], axis=0)
+            out_ref[:, at] = (own_ref[i, :, at] + dot(spread_ref[i], got, 1, 0)).astype(BF16)
+            copies.append(pltpu.make_async_copy(out_ref.at[:, at], hbm.at[:, at], sems.at[len(copies)]))
             copies[-1].start()
     for copy in copies:
         copy.wait()
@@ -384,12 +386,13 @@
     )
     far_got = far_swap(far)
     near_got = near_swap(near)
-    q, gain, scaled, lifted, stats, mix, bias, unfold, fold = call(
+    q, gain, scaled, lifted, stats, mix, bias, unfold, fold, spread = call(
         local_kernel,
         on(VMEM, k, v, mid) + on(HBM, queries, cotangent, gain),
         on(
             VMEM, whole, arr((1, feats), F32), tiles, arr((2, heads, OWN, GROUP), BF16), arr((2, 2 * heads, GROUP), F32),
             tiles, arr((2, RIM, GROUP), F32), arr((2, 2 * SIDE, 2 * PACKED), BF16), arr((2, 2 * PACKED, 2 * SIDE), BF16),
+            arr((2, rows, 2 * SIDE + 2 * PACKED + rows // 4), BF16),
         ),
         [pltpu.VMEM((rows, feats), BF16), pltpu.VMEM((2, OWN, GROUP), F32), dma((3,))],
         10**9,
@@ -416,10 +419,10 @@
     (near_piece,) = call(near_kernel, on(VMEM, q, side_w, ds, dout, fold), on(VMEM, packed), [sides], 10**9)
     near_back = near_swap(near_piece)
     own_tiles = pltpu.VMEM((2, heads, OWN, GROUP), BF16)
-    own, mid_grad, spread, normed, query_grad = call(
+    own, mid_grad, normed, query_grad = call(
         own_kernel,
         on(VMEM, q, k, v, mid, side, gain, lifted, own_scale, attended, sums, ds, dout, delta),
-        on(VMEM, arr((2, rows, feats), F32), mids, arr((2, rows, 2 * SIDE + 2 * PACKED + rows // 4), BF16)) + on(HBM, whole, whole),
+        on(VMEM, arr((2, rows, feats), F32), mids) + on(HBM, whole, whole),
         [pltpu.VMEM((rows, feats), BF16), pltpu.VMEM((rows, feats), BF16), own_tiles, own_tiles, dma((4,))],
         10**6,
     )
@@ -427,7 +430,7 @@
         final_kernel,
         on(VMEM, own, mid_grad, spread, far_back, near_back),
         on(HBM, whole, whole),
-        [pltpu.VMEM((rows, feats), BF16), pltpu.VMEM((rows, feats), BF16), dma((4,))],
+        [pltpu.VMEM((rows, feats), BF16), pltpu.VMEM((rows, feats), BF16), dma((2 * PARTS,))],
         10**8,
     )
     return normed, query_grad, key_grad, value_grad

time: 39.3 us -> 39.3 us (level)
  no operation moved by 1% of the time
where the time goes in v5:
time: 39.3 us; the launch traced here: 39.1 us
  starting transfers between devices  15.2 us (39%)
  Pallas kernels  9.83 us (25%)
  blocking collectives  8.25 us (21%)
  waiting for transfers between devices  5.17 us (13%)
  between operations  0.71 us (2%)
    ppermute x2, starting transfers between devices, far_swap(): return lax.ppermute(x, 'seq', pairs + [(j, i) for i, j in pairs])  11.3 us
    pallas_call x7, Pallas kernels, call(): pl.pallas_call(kernel, out_shape=tuple((shape for shape, _ in outs)), in_...  9.83 us
    all_gather x1, blocking collectives, local(): sums = lax.all_gather(sums, 'head')  8.25 us
    ppermute x2, waiting for transfers between devices, far_swap(): return lax.ppermute(x, 'seq', pairs + [(j, i) for i, j in pairs])  5.16 us
    ppermute x2, starting transfers between devices, near_swap(): return lax.ppermute(x, 'seq', pairs + [(j, i) for i, j in pairs])  3.84 us
  transfers between devices with their start and end apart: 4, of which 2 were waited for; matrix products, arithmetic and copies ran while one was open for 0% of the time, Pallas kernels for 13%

profile of v5, /device:TPU:256, one launch (start us, length us, event | category | flops | bytes accessed | tf_op | source)
XLA Modules:
  0.0 39.1 jit_solution(18361843306852663761)
XLA Ops:
  0.6 1.6 %shard_map.84 = (bf16[256,1024]{1,0:T(8,128)(2,1)S(1)}, bf16[256,1024]{1,0:T(8,128)(2,1)S(1)}, bf16[80,1024]{1,0:T(8,128)(2,1)S(1)}, bf16[80,1024]{1,0:T(8,128)(2,1)S(1)}, bf16[2,64,1024]{2,1,0:T(8,128)(2,1)S(1)}) custom-call(bf16[256,1024]{1,0:T(8,128)(2,1)} %k_hbm.1, bf16[256,1024]{1,0:T(8,128)(2,1)} %v_hbm.1), custom_call_target="tpu_custom_call" | custom-call | flops 100000000 | bytes 390625 | tf_op jit(solution)/shard_map/pallas_call | solution.py:344
  2.2 6.2 %collective-permute-start = (bf16[80,1024]{1,0:T(8,128)(2,1)S(1)}, bf16[80,1024]{1,0:T(8,128)(2,1)S(1)}, u32[]{:S(2)}, u32[]{:S(2)}) collective-permute-start(bf16[80,1024]{1,0:T(8,128)(2,1)S(1)} %get-tuple-element.40), channel_id=1, source_target_pairs={{2,4},{6,8},{10,12},{14,16},{18,20},{22,24},{26,28},{30,32},{34,36... | collective-permute-start | bytes 491528 | tf_op jit(solution)/shard_map/ppermute | solution.py:361
  8.5 1.9 %collective-permute-start.1 = (bf16[80,1024]{1,0:T(8,128)(2,1)S(1)}, bf16[80,1024]{1,0:T(8,128)(2,1)S(1)}, u32[]{:S(2)}, u32[]{:S(2)}) collective-permute-start(bf16[80,1024]{1,0:T(8,128)(2,1)S(1)} %get-tuple-element.41), channel_id=1, source_target_pairs={{0,2},{4,6},{8,10},{12,14},{16,18},{20,22},{24,26},{28,30},{32,34}... | collective-permute-start | bytes 491528 | tf_op jit(solution)/shard_map/ppermute | solution.py:366
  10.4 2.4 %shard_map.85 = (bf16[256,1024]{1,0:T(8,128)(2,1)S(1)}, f32[1,1024]{1,0:T(1,128)S(1)}, f32[2,8,128,128]{3,2,1,0:T(8,128)S(1)}, bf16[2,8,192,128]{3,2,1,0:T(8,128...) custom-call(bf16[256,1024]{1,0:T(8,128)(2,1)S(1)} %get-tuple-element, ...), custom_call_target="tpu_custom_call" | custom-call | flops 1000000000 | bytes 3906250 | tf_op jit(solution)/shard_map/pallas_call | solution.py:344
  12.8 2.1 %collective-permute-done.far_ref = bf16[80,1024]{1,0:T(8,128)(2,1)S(1)} collective-permute-done((bf16[80,1024]{1,0:T(8,128)(2,1)S(1)}, bf16[80,1024]{1,0:T(8,128)(2,1)S(1)}, u32[]{:S(2)}, u32[]{:S(2)}) %collective-permute-start) | collective-permute-done | bytes 163872 | tf_op jit(solution)/shard_map/ppermute | solution.py:361
  14.9 0.0 collective-permute-done.1.near_ref
  14.9 1.1 %shard_map.86 = (bf16[2,96,1024]{2,1,0:T(8,128)(2,1)S(1)}, bf16[2,8,64,128]{3,2,1,0:T(8,128)(2,1)S(1)}, f32[2,8,128]{2,1,0:T(8,128)S(1)}, f32[2,8,128]{2,1,0:T(8...) custom-call(bf16[256,1024]{1,0:T(8,128)(2,1)S(1)} %get-tuple-element.39.q_ref, ...), custom_call_target="tpu_custom_call" | custom-call | flops 1000000000 | bytes 3906250 | tf_op jit(solution)/shard_map/pallas_call | solution.py:344
  15.9 8.2 %all-gather.1.sums_ref = f32[2,2,256]{2,1,0:T(2,128)S(1)} all-gather(f32[1,2,256]{2,1,0:T(2,128)S(1)} %bitcast.2), channel_id=2, replica_groups=mesh['seq'=256,'head'=2] {'head'}, dimensions={0}, use_global_device_ids=true | all-gather | bytes 6144 | tf_op jit(solution)/shard_map/all_gather | solution.py:410
  24.2 0.7 %shard_map.87 = (bf16[96,1024]{1,0:T(8,128)(2,1)S(1)}, bf16[2,8,64,128]{3,2,1,0:T(8,128)(2,1)S(1)}, bf16[2,8,64,128]{3,2,1,0:T(8,128)(2,1)S(1)}, bf16[2,8,128,128]{3,2,1,0:T(8,128)(2,1)S(1)}, f32[2,8,128]{2,1,0:T(8,128)S(1)}) custom-call(bf16[256,1024]{1,0:T(8,128)(2,1)S(1)} %get-tuple-element.39.q_ref, bf16[2,96,1024]{2,1,0:T(8,128)(2,1)S(1)} %get-tuple-element.47.side_ref, ...), custom_call_target="tpu_custom_call" | custom-call | flops 1000000000 | bytes 3906250 | tf_op jit(solution)/shard_map/pallas_call | solution.py:344
  24.9 5.1 %collective-permute-start.2 = (bf16[96,1024]{1,0:T(8,128)(2,1)S(1)}, bf16[96,1024]{1,0:T(8,128)(2,1)S(1)}, u32[]{:S(2)}, u32[]{:S(2)}) collective-permute-start(bf16[96,1024]{1,0:T(8,128)(2,1)S(1)} %get-tuple-element.63), channel_id=1, source_target_pairs={{2,4},{6,8},{10,12},{14,16},{18,20},{22,24},{26,28},{30,32},{34,36... | collective-permute-start | bytes 589832 | tf_op jit(solution)/shard_map/ppermute | solution.py:361
  30.0 0.6 %shard_map.89 = bf16[80,1024]{1,0:T(8,128)(2,1)S(1)} custom-call(bf16[256,1024]{1,0:T(8,128)(2,1)S(1)} %get-tuple-element.39.q_ref, bf16[2,8,64,128]{3,2,1,0:T(8,128)(2,1)S(1)} %get-tuple-element.64.side_w, bf16[2,8,64,128]{3,2,1,0:T(8,128)(2,1)S(1)} %get-tuple-element.55.ds_ref, bf16[2,8,128,128]{3,2,1,0:T(8,128)(2,1)S(1)} %get-tuple-element.56.dout_ref, ...), custom_call_target="tpu_custom_call" | custom-call | flops 1000000000 | bytes 3906250 | tf_op jit(solution)/shard_map/pallas_call | solution.py:344
  30.5 1.9 %collective-permute-start.3 = (bf16[80,1024]{1,0:T(8,128)(2,1)S(1)}, bf16[80,1024]{1,0:T(8,128)(2,1)S(1)}, u32[]{:S(2)}, u32[]{:S(2)}) collective-permute-start(bf16[80,1024]{1,0:T(8,128)(2,1)S(1)} %shard_map.89), channel_id=1, source_target_pairs={{0,2},{4,6},{8,10},{12,14},{16,18},{20,22},{24,26},{28,30},{32,34}... | collective-permute-start | bytes 491528 | tf_op jit(solution)/shard_map/ppermute | solution.py:366
  32.5 2.3 %shard_map.88 = (f32[2,256,1024]{2,1,0:T(8,128)S(1)}, bf16[2,64,1024]{2,1,0:T(8,128)(2,1)S(1)}, bf16[256,1024]{1,0:T(8,128)(2,1)}, bf16[256,1024]{1,0:T(8,128)(2,1)}) custom-call(bf16[256,1024]{1,0:T(8,128)(2,1)S(1)} %get-tuple-element.39.q_ref, bf16[256,1024]{1,0:T(8,128)(2,1)S(1)} %get-tuple-element.36.k_ref, ...), custom_call_target="tpu_custom_call" | custom-call | flops 1000000 | bytes 3906 | tf_op jit(solution)/shard_map/pallas_call | solution.py:344
  34.8 0.0 collective-permute-done.3.near_ref
  34.8 3.1 %collective-permute-done.2.far_ref = bf16[96,1024]{1,0:T(8,128)(2,1)S(1)} collective-permute-done((bf16[96,1024]{1,0:T(8,128)(2,1)S(1)}, bf16[96,1024]{1,0:T(8,128)(2,1)S(1)}, u32[]{:S(2)}, u32[]{:S(2)}) %collective-permute-start.2) | collective-permute-done | bytes 196640 | tf_op jit(solution)/shard_map/ppermute | solution.py:361
  37.9 1.2 %shard_map.90 = (bf16[256,1024]{1,0:T(8,128)(2,1)}, bf16[256,1024]{1,0:T(8,128)(2,1)}) custom-call(f32[2,256,1024]{2,1,0:T(8,128)S(1)} %get-tuple-element.60.own_ref, bf16[2,64,1024]{2,1,0:T(8,128)(2,1)S(1)} %get-tuple-element.61.mid_grad, bf16[2,256,240]{2,1,0:T(8,128)(2,1)S(1)} %get-tuple-element.62.spread_ref, ...), custom_call_target="tpu_custom_call" | custom-call | flops 100000000 | bytes 390625 | tf_op jit(solution)/shard_map/pallas_call | solution.py:344
Async XLA Ops:
  2.2 12.7 %collective-permute-start = (bf16[80,1024]{1,0:T(8,128)(2,1)S(1)}, bf16[80,1024]{1,0:T(8,128)(2,1)S(1)}, u32[]{:S(2)}, u32[]{:S(2)}) collective-permute-start(bf16[80,1024]{1,0:T(8,128)(2,1)S(1)} %get-tuple-element.40), channel_id=1, source_target_pairs={{2,4},{6,8},{10,12},{14,16},{18,20},{22,24},{26,28},{30,32},{34,36... | collective-permute-start | bytes 491528 | tf_op jit(solution)/shard_map/ppermute | solution.py:361
  8.5 6.4 %collective-permute-start.1 = (bf16[80,1024]{1,0:T(8,128)(2,1)S(1)}, bf16[80,1024]{1,0:T(8,128)(2,1)S(1)}, u32[]{:S(2)}, u32[]{:S(2)}) collective-permute-start(bf16[80,1024]{1,0:T(8,128)(2,1)S(1)} %get-tuple-element.41), channel_id=1, source_target_pairs={{0,2},{4,6},{8,10},{12,14},{16,18},{20,22},{24,26},{28,30},{32,34}... | collective-permute-start | bytes 491528 | tf_op jit(solution)/shard_map/ppermute | solution.py:366
  24.9 13.0 %collective-permute-start.2 = (bf16[96,1024]{1,0:T(8,128)(2,1)S(1)}, bf16[96,1024]{1,0:T(8,128)(2,1)S(1)}, u32[]{:S(2)}, u32[]{:S(2)}) collective-permute-start(bf16[96,1024]{1,0:T(8,128)(2,1)S(1)} %get-tuple-element.63), channel_id=1, source_target_pairs={{2,4},{6,8},{10,12},{14,16},{18,20},{22,24},{26,28},{30,32},{34,36... | collective-permute-start | bytes 589832 | tf_op jit(solution)/shard_map/ppermute | solution.py:361
  30.5 4.2 %collective-permute-start.3 = (bf16[80,1024]{1,0:T(8,128)(2,1)S(1)}, bf16[80,1024]{1,0:T(8,128)(2,1)S(1)}, u32[]{:S(2)}, u32[]{:S(2)}) collective-permute-start(bf16[80,1024]{1,0:T(8,128)(2,1)S(1)} %shard_map.89), channel_id=1, source_target_pairs={{0,2},{4,6},{8,10},{12,14},{16,18},{20,22},{24,26},{28,30},{32,34}... | collective-permute-start | bytes 491528 | tf_op jit(solution)/shard_map/ppermute | solution.py:366
